TPU v7x, 32 devices: a whole 2x2x4 slice. The times are simulated.
32 devices in a mesh: dp: 16 (over z, x, core), head: 2 (over y).
Axes of the slice: x: 2, y: 2, z: 4, core: 2. Of those that a mesh axis runs over, the one named last changes fastest.
Arguments:
- inputs: float32 [1024, 16, 512], P('head', 'dp'), may hold values from -6 to 6
- doc_starts: int32 [16, 4], P('dp'), may hold values from 0 to 1023, as said below
- query_weight: float32 [512, 512], P(None, 'head'), may hold values from -1 to 1
- key_weight: float32 [512, 512], P(None, 'head'), may hold values from -0.25 to 0.25
- value_weight: float32 [512, 512], P(None, 'head'), may hold values from -0.25 to 0.25
- control_weight: float32 [512, 512], P(None, 'head'), may hold values from -0.5 to 0.5
- output_weight: float32 [512, 512], P('head'), may hold values from -2 to 2
- up_weight: float32 [512, 2048], P(None, 'head'), may hold values from -0.25 to 0.25
- down_weight: float32 [2048, 512], P('head'), may hold values from -0.125 to 0.125
- first_gain: float32 [512], replicated, may hold values from 0.5 to 1.5
- first_shift: float32 [512], replicated, may hold values from -2 to 2
- second_gain: float32 [512], replicated, may hold values from 0.5 to 1.5
- second_shift: float32 [512], replicated, may hold values from -2 to 2
- cotangent: float32 [1024, 16, 512], P('head', 'dp'), may hold values from -6 to 6
Outputs:
- outputs: float32 [1024, 16, 512], P('head', 'dp')
- grad_inputs: float32 [1024, 16, 512], P('head', 'dp')
- grad_query: float32 [512, 512], P(None, 'head')
- grad_key: float32 [512, 512], P(None, 'head')
- grad_value: float32 [512, 512], P(None, 'head')
- grad_control: float32 [512, 512], P(None, 'head')
- grad_output: float32 [512, 512], P('head')
- grad_up: float32 [512, 2048], P(None, 'head')
- grad_down: float32 [2048, 512], P('head')
- grad_first_gain: float32 [512], replicated
- grad_first_shift: float32 [512], replicated
- grad_second_gain: float32 [512], replicated
- grad_second_shift: float32 [512], replicated
Inputs may be any that keep to these rules, and one draw needn't show every extreme that they name: `doc_starts`: each row holds 4 strictly rising document starts, the first 0; one document of each row begins before position 512 and ends after it.
All inputs are finite; a program needn't handle non-finite values.
Results may differ from a plain program's by a relative error of at most 0.0003.
Values sent between devices are 32-bit elements; how exact they have to be, the bound alone decides.
No kernel may reach another device: no remote copies, remote signals or barrier semaphores. Data moves between devices by JAX's collectives and lax.ppermute only.
A program may use at most 128 MiB of HBM per device.

v0:
```python
from functools import partial

import jax
import jax.numpy as jnp
from jax import lax
from jax.sharding import PartitionSpec as P

HD = 64
SLOTS = 64


precise = lax.Precision.HIGHEST


def product(left, right):
    return jnp.dot(left, right, precision=precise, preferred_element_type=jnp.float32)


def outer_sum(left, right):
    return jnp.einsum(
        "rsi,rsj->ij", left, right, precision=precise, preferred_element_type=jnp.float32
    )


def layer_norm(values, gain, shift):
    centre = values - jnp.mean(values, axis=-1, keepdims=True)
    spread = jnp.mean(centre * centre, axis=-1, keepdims=True)
    return centre * lax.rsqrt(spread + 1e-05) * gain + shift


def slot_attention(query_rows, key_rows, value_rows, control_rows, doc_ids):
    length = query_rows.shape[0]
    position = jnp.arange(length, dtype=jnp.int32)
    allowed = (
        (position[:, None] >= position[None, :]) & (doc_ids[:, None] == doc_ids[None, :])
    ).astype(jnp.float32)
    control_exp = jnp.exp(control_rows)
    totals = product(allowed, control_exp)
    affinity = allowed * product(query_rows, key_rows.T)
    scores = product(affinity, control_exp) / totals * query_rows.shape[-1] ** (-0.5)
    probs = jax.nn.softmax(scores, axis=-1)
    mixing = allowed * product(probs / totals, control_exp.T)
    return product(mixing, value_rows)


def to_entries(tensor, per_head):
    length, seq_count, col_count = tensor.shape
    head_count = col_count // per_head
    return (
        tensor.reshape(length, seq_count, head_count, per_head)
        .transpose(1, 2, 0, 3)
        .reshape(seq_count * head_count, length, per_head)
    )


def from_entries(entries, seq_count):
    entry_count, length, per_head = entries.shape
    head_count = entry_count // seq_count
    return (
        entries.reshape(seq_count, head_count, length, per_head)
        .transpose(2, 0, 1, 3)
        .reshape(length, seq_count, head_count * per_head)
    )


def attention_back(entry):
    query_rows, key_rows, value_rows, control_rows, doc_ids, output_grad = entry

    def local_attention(query_part, key_part, value_part, control_part):
        return slot_attention(query_part, key_part, value_part, control_part, doc_ids)

    _, pullback = jax.vjp(local_attention, query_rows, key_rows, value_rows, control_rows)
    return pullback(output_grad)


def per_device(
    inputs,
    doc_starts,
    query_weight,
    key_weight,
    value_weight,
    control_weight,
    output_weight,
    up_weight,
    down_weight,
    first_gain,
    first_shift,
    second_gain,
    second_shift,
    cotangent,
):
    rows_here = inputs.shape[0]
    seq_count = inputs.shape[1]
    model_width = inputs.shape[2]
    head_width = query_weight.shape[1]
    length = rows_here * lax.axis_size("head")
    packed = jnp.concatenate([query_weight, key_weight, value_weight, control_weight], axis=1)
    normed = layer_norm(inputs, first_gain, first_shift)
    row_piece = lax.all_gather(normed, "head", axis=0, tiled=True)
    joined_first = jnp.concatenate([row_piece, product(row_piece, packed)], axis=2)
    gathered_first = joined_first[:, :, :model_width]
    projected = joined_first[:, :, model_width:]
    query_rows = projected[:, :, :head_width]
    key_rows = projected[:, :, head_width : 2 * head_width]
    value_rows = projected[:, :, 2 * head_width : 3 * head_width]
    control_rows = projected[:, :, 3 * head_width :]
    position = jnp.arange(length, dtype=jnp.int32)
    doc_ids = jnp.sum((doc_starts[:, None, :] <= position[None, :, None]).astype(jnp.int32), axis=2)
    head_count = head_width // HD
    doc_entries = jnp.repeat(doc_ids, head_count, axis=0)
    entries = (
        to_entries(query_rows, HD),
        to_entries(key_rows, HD),
        to_entries(value_rows, HD),
        to_entries(control_rows, SLOTS),
        doc_entries,
    )

    def attention_forward(entry):
        return slot_attention(entry[0], entry[1], entry[2], entry[3], entry[4])

    attended = from_entries(lax.map(attention_forward, entries), seq_count)
    hidden_state = inputs + lax.psum_scatter(
        product(attended, output_weight), "head", scatter_dimension=0, tiled=True
    )
    second = layer_norm(hidden_state, second_gain, second_shift)
    row_piece = lax.all_gather(second, "head", axis=0, tiled=True)
    joined_second = jnp.concatenate([row_piece, product(row_piece, up_weight)], axis=2)
    gathered_second = joined_second[:, :, :model_width]
    upper = joined_second[:, :, model_width:]
    activated = jax.nn.gelu(upper, approximate=True)
    outputs = hidden_state + lax.psum_scatter(
        product(activated, down_weight), "head", scatter_dimension=0, tiled=True
    )
    row_piece = lax.all_gather(cotangent, "head", axis=0, tiled=True)
    joined_back = jnp.concatenate([row_piece, product(row_piece, down_weight.T)], axis=2)
    full_cotangent = joined_back[:, :, :model_width]
    d_activated = joined_back[:, :, model_width:]
    grad_down = outer_sum(activated, full_cotangent)
    _, gelu_back = jax.vjp(partial(jax.nn.gelu, approximate=True), upper)
    d_upper = gelu_back(d_activated)[0]
    grad_up = outer_sum(gathered_second, d_upper)
    d_second = lax.psum_scatter(
        product(d_upper, up_weight.T), "head", scatter_dimension=0, tiled=True
    )
    _, second_norm_back = jax.vjp(layer_norm, hidden_state, second_gain, second_shift)
    d_hidden_norm, grad_second_gain, grad_second_shift = second_norm_back(d_second)
    d_hidden = cotangent + d_hidden_norm
    row_piece = lax.all_gather(d_hidden, "head", axis=0, tiled=True)
    joined_hidden = jnp.concatenate([row_piece, product(row_piece, output_weight.T)], axis=2)
    full_hidden = joined_hidden[:, :, :model_width]
    d_attended = joined_hidden[:, :, model_width:]
    grad_output = outer_sum(attended, full_hidden)
    back_entries = lax.map(attention_back, entries + (to_entries(d_attended, HD),))
    d_projected = jnp.concatenate(
        [from_entries(member, seq_count) for member in back_entries], axis=2
    )
    grad_packed = outer_sum(gathered_first, d_projected)
    grad_query = grad_packed[:, :head_width]
    grad_key = grad_packed[:, head_width : 2 * head_width]
    grad_value = grad_packed[:, 2 * head_width : 3 * head_width]
    grad_control = grad_packed[:, 3 * head_width :]
    d_first = lax.psum_scatter(
        product(d_projected, packed.T), "head", scatter_dimension=0, tiled=True
    )
    _, first_norm_back = jax.vjp(layer_norm, inputs, first_gain, first_shift)
    d_input_norm, grad_first_gain, grad_first_shift = first_norm_back(d_first)
    grad_inputs = d_hidden + d_input_norm
    gain_stack = jnp.stack([grad_first_gain, grad_first_shift, grad_second_gain, grad_second_shift])
    grad_query, grad_key, grad_value, grad_control, grad_output, grad_up, grad_down = lax.psum(
        (grad_query, grad_key, grad_value, grad_control, grad_output, grad_up, grad_down), "dp"
    )
    gain_stack = lax.psum(gain_stack, ("dp", "head"))
    return (
        outputs,
        grad_inputs,
        grad_query,
        grad_key,
        grad_value,
        grad_control,
        grad_output,
        grad_up,
        grad_down,
        gain_stack[0],
        gain_stack[1],
        gain_stack[2],
        gain_stack[3],
    )


def solution(mesh):
    return jax.shard_map(
        per_device,
        mesh=mesh,
        in_specs=(
            P("head", "dp", None),
            P("dp", None),
            P(None, "head"),
            P(None, "head"),
            P(None, "head"),
            P(None, "head"),
            P("head", None),
            P(None, "head"),
            P("head", None),
            P(),
            P(),
            P(),
            P(),
            P("head", "dp", None),
        ),
        out_specs=(
            P("head", "dp", None),
            P("head", "dp", None),
            P(None, "head"),
            P(None, "head"),
            P(None, "head"),
            P(None, "head"),
            P("head", None),
            P(None, "head"),
            P("head", None),
            P(),
            P(),
            P(),
            P(),
        ),
        check_vma=False,
    )
```

profile of v0, /device:TPU:0, one launch (start us, length us, event | category | flops | bytes accessed | tf_op | source)
XLA Modules:
  0.0 827.6 jit_solution(11557536122245836172)
XLA Ops:
  20.8 30.4 %all-gather.5.cloned.1.call-done = f32[1024,1,512]{2,0,1:T(8,128)} async-done(((f32[512,1,512]{2,0,1:T(8,128)}), f32[1024,1,512]{2,0,1:T(8,128)}) %all-gather.5.cloned.1.call-update) | async-done | bytes 2097168 | tf_op jit(solution)/shard_map/all_gather | solution.py:99
  51.2 9.0 %convolution_bitcast_fusion = f32[1024,1,1024]{0,2,1:T(8,128)S(1)} fusion(f32[512,1024]{1,0:T(8,128)} %constant_dynamic-update-slice_fusion, f32[1024,1,512]{2,0,1:T(8,128)} %all-gather.5.cloned.1.call-done), kind=kOutput, calls=%fused_computation.154 | convolution fusion | flops 6442450944 | bytes 8388608 | tf_op jit(solution)/shard_map/dot_general | solution.py:16
  72.5 77.9 %while.26 = (s32[]{:T(128)}, f32[4,1024,64]{1,2,0:T(8,128)}, s32[4,1024]{1,0:T(4,128)S(1)}, f32[4,1024,64]{2,1,0:T(8,128)}, f32[4,1024,64]{2,1,0:T(8,128)}, /*in...) while((s32[]{:T(128)}, f32[4,1024,64]{1,2,0:T(8,128)}, s32[4,1024]{1,0:T(4,128)S(1)}, ...), condition=%wide.region_6.7_spmd, body=%wide.region_3.6_spmd.sunk | while | flops 4038588416 | bytes 30455964 | solution.py:122
  87.3 5.0 fusion.288
  106.7 5.0 fusion.288
  126.0 5.0 fusion.288
  145.3 5.0 fusion.288
  155.1 31.9 %reduce-scatter.5.cloned.1.call-done = f32[512,1,512]{2,0,1:T(8,128)} async-done(((f32[1024,1,512]{2,0,1:T(8,128)}), f32[512,1,512]{2,0,1:T(8,128)}) %reduce-scatter.5.cloned.1.call-update) | async-done | bytes 1048592 | tf_op jit(solution)/shard_map/reduce_scatter | solution.py:123
  191.7 32.6 %all-gather.7.cloned.1.call-done = f32[1024,1,512]{2,0,1:T(8,128)} async-done(((f32[512,1,512]{2,0,1:T(8,128)}), f32[1024,1,512]{2,0,1:T(8,128)}) %all-gather.7.cloned.1.call-update) | async-done | bytes 2097168 | tf_op jit(solution)/shard_map/all_gather | solution.py:127
  224.3 9.7 %fusion.184 = f32[1024,1024]{1,0:T(8,128)} fusion(f32[512,1024]{1,0:T(8,128)S(1)} %copy-done, f32[1024,1,512]{2,0,1:T(8,128)} %all-gather.7.cloned.1.call-done), kind=kOutput, calls=%fused_computation.164 | convolution fusion | flops 6442450944 | bytes 8388608 | tf_op jit(solution)/shard_map/dot_general | solution.py:16
  234.0 24.9 %all-gather.9.cloned.1.call-done = f32[1024,1,512]{2,1,0:T(1,128)} async-done(((f32[512,1,512]{2,1,0:T(1,128)}), f32[1024,1,512]{2,1,0:T(1,128)}) %all-gather.9.cloned.1.call-update) | async-done | bytes 2097168 | tf_op jit(solution)/shard_map/all_gather | solution.py:135
  258.9 13.0 %fusion.172 = f32[1024,1024]{1,0:T(8,128)S(1)} fusion(f32[1024,1024]{1,0:T(8,128)} %fusion.184, f32[1024,512]{1,0:T(8,128)} %param.26, f32[1024,1,512]{2,1,0:T(1,128)} %all-gather.9.cloned.1.call-done), kind=kOutput, calls=%fused_computation.149 | convolution fusion | flops 6462373888 | bytes 12582912 | tf_op jit(solution)/shard_map/dot_general | solution.py:16
  273.9 8.0 convolution_bitcast_fusion.2
  282.0 11.4 %fusion.191 = f32[1024,1,512]{2,0,1:T(8,128)} fusion(f32[1024,512]{1,0:T(8,128)} %param.26, f32[1024,1024]{1,0:T(8,128)} %fusion.184), kind=kOutput, calls=%fused_computation.172 | convolution fusion | flops 6450839552 | bytes 8388608 | tf_op jit(solution)/shard_map/dot_general | solution.py:16
  293.5 20.4 %reduce-scatter.9.cloned.1.call-done = f32[512,1,512]{2,0,1:T(8,128)} async-done(((f32[1024,1,512]{2,0,1:T(8,128)}), f32[512,1,512]{2,0,1:T(8,128)}) %reduce-scatter.9.cloned.1.call-update) | async-done | bytes 1048592 | tf_op jit(solution)/shard_map/reduce_scatter | solution.py:143
  315.6 32.3 %reduce-scatter.7.cloned.1.call-done = f32[512,1,512]{2,0,1:T(8,128)} async-done(((f32[1024,1,512]{2,0,1:T(8,128)}), f32[512,1,512]{2,0,1:T(8,128)}) %reduce-scatter.7.cloned.1.call-update) | async-done | bytes 1048592 | tf_op jit(solution)/shard_map/reduce_scatter | solution.py:132
  353.2 33.2 %all-gather.11.cloned.1.call-done = f32[1024,1,512]{2,0,1:T(8,128)} async-done(((f32[512,1,512]{2,0,1:T(8,128)}), f32[1024,1,512]{2,0,1:T(8,128)}) %all-gather.11.cloned.1.call-update) | async-done | bytes 2097168 | tf_op jit(solution)/shard_map/all_gather | solution.py:149
  394.6 208.9 %while.27 = (s32[]{:T(128)}, f32[4,1024,64]{1,2,0:T(8,128)}, f32[4,1024,64]{1,2,0:T(8,128)}, f32[4,1024,64]{1,2,0:T(8,128)}, f32[4,1024,64]{1,2,0:T(8,128)}, /*i...) while((s32[]{:T(128)}, f32[4,1024,64]{1,2,0:T(8,128)}, ...), condition=%wide.region_18.19_spmd, body=%wide.region_14.0_spmd.sunk | while | flops 10504568832 | bytes 67015888 | solution.py:154
  418.7 5.0 convolution_select_fusion.2
  450.5 5.0 fusion.315
  463.5 5.0 convolution_select_fusion.2
  495.3 5.0 fusion.315
  508.2 5.0 convolution_select_fusion.2
  540.1 5.0 fusion.315
  553.0 5.0 convolution_select_fusion.2
  584.8 5.0 fusion.315
  603.5 16.8 %fusion.192 = f32[1024,1,512]{2,0,1:T(8,128)} fusion(f32[512,1024]{1,0:T(8,128)} %constant_dynamic-update-slice_fusion, f32[1024,1,256]{0,2,1:T(8,128)} %bitcast.253, f32[1024,1,256]{0,2,1:T(8,128)} %bitcast.255, f32[1024,1,256]{0,2,1:T(8,128)} %bitcast.257, f32[1024,1,256]{0,2,1:T(8,128)} %bitcast.259), kind=kOutput, calls=%fused_computation.173 | convolution fusion | flops 6445596672 | bytes 8388608 | tf_op jit(solution)/shard_map/dot_general | solution.py:16
  620.4 9.9 %fusion.182 = f32[512,1024]{1,0:T(8,128)} fusion(f32[1024,1024]{1,0:T(8,128)} %copy-done.7, f32[1024,1,512]{2,0,1:T(8,128)S(1)} %copy-done.8), kind=kOutput, calls=%fused_computation.162 | convolution fusion | flops 6442450944 | bytes 8388608 | tf_op jit(solution)/shard_map/rsi,rsj->ij/dot_general | solution.py:20
  630.4 9.0 %fusion.175 = f32[1024,512]{1,0:T(8,128)} fusion(f32[1024,1,512]{2,1,0:T(1,128)S(1)} %copy-done.36, f32[1024,1024]{1,0:T(8,128)S(1)} %copy-done.15), kind=kOutput, calls=%fused_computation.155 | convolution fusion | flops 6450839552 | bytes 8388608 | tf_op jit(solution)/shard_map/rsi,rsj->ij/dot_general | solution.py:20
  639.5 13.6 %fusion.173 = f32[512,1024]{1,0:T(8,128)S(1)} fusion(f32[1024,1,256]{0,2,1:T(8,128)S(1)} %bitcast.254, f32[1024,1,256]{0,2,1:T(8,128)S(1)} %bitcast.256, f32[1024,1,256]{0,2,1:T(8,128)S(1)} %bitcast.258, f32[1024,1,256]{0,2,1:T(8,128)S(1)} %bitcast.260, f32[1024,1,512]{2,0,1:T(8,128)S(1)} %copy-done.35), kind=kOutput, calls=%fused_computation.152 | convolution fusion | flops 6445596672 | bytes 8388608 | tf_op jit(solution)/shard_map/rsi,rsj->ij/dot_general | solution.py:20
  667.8 41.3 %psum.63 = f32[4,512]{1,0:T(4,128)S(1)} all-reduce(f32[4,512]{1,0:T(4,128)S(1)} %pad_maximum_fusion), channel_id=1, replica_groups=mesh['dp'=16,'head'=2] {'dp','head'}, use_global_device_ids=true, to_apply=%region_33.34 | all-reduce | flops 2048 | bytes 16384 | tf_op jit(solution)/shard_map/psum | solution.py:173
  709.7 100.0 %all-reduce.3.cloned.1.call-done = (f32[512,256]{1,0:T(8,128)}, f32[512,256]{1,0:T(8,128)}, f32[512,256]{1,0:T(8,128)}, f32[512,256]{1,0:T(8,128)}, f32[256,512]...) async-done(((f32[512,256]{1,0:T(8,128)}, f32[512,256]{1,0:T(8,128)}, f32[512,256]{1,0:T(8,128)}, f32[512,256]{1,0:T(8,128)}, f32[256,512]{1,0:T(8,128)}, ...) | async-done | bytes 6815760 | tf_op jit(solution)/shard_map/psum | solution.py:170
  (259 shorter events, 274.8 us)
Async XLA Ops:
  7.2 217.1 %copy-start = (f32[512,1024]{1,0:T(8,128)S(1)}, f32[512,1024]{1,0:T(8,128)}, u32[]{:S(2)}) copy-start(f32[512,1024]{1,0:T(8,128)} %param.25) | copy-start | bytes 6291460
  7.2 8.2 copy-start.22
  7.2 9.0 %copy-start.23 = (f32[512,256]{1,0:T(8,128)S(1)}, f32[512,256]{1,0:T(8,128)}, u32[]{:S(2)}) copy-start(f32[512,256]{1,0:T(8,128)} %param.21) | copy-start | bytes 1572868
  7.2 44.0 %all-gather.5.cloned.1.call-start = ((), (), s32[]{:S(2)}) async-start(), calls=%async_computation.4 | async-start | bytes 3145728 | tf_op jit(solution)/shard_map/all_gather | solution.py:99
  15.2 171.8 %reduce-scatter.5.cloned.1.call-start = ((), (), s32[]{:S(2)}) async-start(), calls=%async_computation.5 | async-start | bytes 3145728 | tf_op jit(solution)/shard_map/reduce_scatter | solution.py:123
  150.5 39.3 %copy-start.31 = (f32[512]{0:T(512)S(1)}, f32[512]{0:T(512)}, u32[]{:S(2)}) copy-start(f32[512]{0:T(512)} %param.29) | copy-start | bytes 6148
  150.5 39.3 %copy-start.33 = (f32[512]{0:T(512)S(1)}, f32[512]{0:T(512)}, u32[]{:S(2)}) copy-start(f32[512]{0:T(512)} %param.30) | copy-start | bytes 6148
  155.1 69.2 %all-gather.7.cloned.1.call-start = ((), (), s32[]{:S(2)}) async-start(), calls=%async_computation.6 | async-start | bytes 3145728 | tf_op jit(solution)/shard_map/all_gather | solution.py:127
  191.0 67.9 %all-gather.9.cloned.1.call-start = ((), (), s32[]{:S(2)}) async-start(), calls=%async_computation.8 | async-start | bytes 3145728 | tf_op jit(solution)/shard_map/all_gather | solution.py:135
  191.6 122.3 %reduce-scatter.9.cloned.1.call-start = ((), (), s32[]{:S(2)}) async-start(), calls=%async_computation.9 | async-start | bytes 3145728 | tf_op jit(solution)/shard_map/reduce_scatter | solution.py:143
  281.9 32.0 %copy-start.6 = (f32[512,1,512]{2,0,1:T(8,128)S(1)}, f32[512,1,512]{2,0,1:T(8,128)}, u32[]{:S(2)}) copy-start(f32[512,1,512]{2,0,1:T(8,128)} %copy-done.5) | copy-start | bytes 3145732
  281.9 65.9 %reduce-scatter.7.cloned.1.call-start = ((), (), s32[]{:S(2)}) async-start(), calls=%async_computation.7 | async-start | bytes 3145728 | tf_op jit(solution)/shard_map/reduce_scatter | solution.py:132
  293.4 93.0 %all-gather.11.cloned.1.call-start = ((), (), s32[]{:S(2)}) async-start(), calls=%async_computation.10 | async-start | bytes 3145728 | tf_op jit(solution)/shard_map/all_gather | solution.py:149
  353.2 308.6 %reduce-scatter.11.cloned.1.call-start = ((), (), s32[]{:S(2)}) async-start(), calls=%async_computation.11 | async-start | bytes 3145728 | tf_op jit(solution)/shard_map/reduce_scatter | solution.py:163
  417.1 10.9 %copy-start.12 = (f32[4,1024,64]{1,2,0:T(8,128)}, f32[4,1024,64]{1,2,0:T(8,128)S(1)}, u32[]{:S(2)}) copy-start(f32[4,1024,64]{1,2,0:T(8,128)S(1)} %get-tuple-element.458) | copy-start | bytes 3145732 | tf_op jit(solution)/shard_map/while
  450.5 8.5 %copy-start.13 = (f32[4,1024,64]{1,2,0:T(8,128)S(1)}, f32[4,1024,64]{1,2,0:T(8,128)}, u32[]{:S(2)}) copy-start(f32[4,1024,64]{1,2,0:T(8,128)} %copy-done.12) | copy-start | bytes 3145732 | tf_op jit(solution)/shard_map/while
  461.9 10.9 %copy-start.12 = (f32[4,1024,64]{1,2,0:T(8,128)}, f32[4,1024,64]{1,2,0:T(8,128)S(1)}, u32[]{:S(2)}) copy-start(f32[4,1024,64]{1,2,0:T(8,128)S(1)} %get-tuple-element.458) | copy-start | bytes 3145732 | tf_op jit(solution)/shard_map/while
  495.3 8.5 %copy-start.13 = (f32[4,1024,64]{1,2,0:T(8,128)S(1)}, f32[4,1024,64]{1,2,0:T(8,128)}, u32[]{:S(2)}) copy-start(f32[4,1024,64]{1,2,0:T(8,128)} %copy-done.12) | copy-start | bytes 3145732 | tf_op jit(solution)/shard_map/while
  506.7 10.9 %copy-start.12 = (f32[4,1024,64]{1,2,0:T(8,128)}, f32[4,1024,64]{1,2,0:T(8,128)S(1)}, u32[]{:S(2)}) copy-start(f32[4,1024,64]{1,2,0:T(8,128)S(1)} %get-tuple-element.458) | copy-start | bytes 3145732 | tf_op jit(solution)/shard_map/while
  540.0 8.5 %copy-start.13 = (f32[4,1024,64]{1,2,0:T(8,128)S(1)}, f32[4,1024,64]{1,2,0:T(8,128)}, u32[]{:S(2)}) copy-start(f32[4,1024,64]{1,2,0:T(8,128)} %copy-done.12) | copy-start | bytes 3145732 | tf_op jit(solution)/shard_map/while
  551.5 10.8 %copy-start.12 = (f32[4,1024,64]{1,2,0:T(8,128)}, f32[4,1024,64]{1,2,0:T(8,128)S(1)}, u32[]{:S(2)}) copy-start(f32[4,1024,64]{1,2,0:T(8,128)S(1)} %get-tuple-element.458) | copy-start | bytes 3145732 | tf_op jit(solution)/shard_map/while
  584.8 8.5 %copy-start.13 = (f32[4,1024,64]{1,2,0:T(8,128)S(1)}, f32[4,1024,64]{1,2,0:T(8,128)}, u32[]{:S(2)}) copy-start(f32[4,1024,64]{1,2,0:T(8,128)} %copy-done.12) | copy-start | bytes 3145732 | tf_op jit(solution)/shard_map/while
  603.5 16.9 %copy-start.8 = (f32[1024,1,512]{2,0,1:T(8,128)S(1)}, f32[1024,1,512]{2,0,1:T(8,128)}, u32[]{:S(2)}) copy-start(f32[1024,1,512]{2,0,1:T(8,128)} %all-gather.7.cloned.1.call-done) | copy-start | bytes 6291460
  620.3 189.3 %all-reduce.3.cloned.1.call-start = ((), (), s32[]{:S(2)}) async-start(), calls=%async_computation.12 | async-start | bytes 13631488 | tf_op jit(solution)/shard_map/psum | solution.py:170
  620.4 9.9 %copy-start.15 = (f32[1024,1024]{1,0:T(8,128)S(1)}, f32[1024,1024]{1,0:T(8,128)}, u32[]{:S(2)}) copy-start(f32[1024,1024]{1,0:T(8,128)} %fusion.184) | copy-start | bytes 12582916
  620.4 9.9 %copy-start.36 = (f32[1024,1,512]{2,1,0:T(1,128)S(1)}, f32[1024,1,512]{2,1,0:T(1,128)}, u32[]{:S(2)}) copy-start(f32[1024,1,512]{2,1,0:T(1,128)} %all-gather.9.cloned.1.call-done) | copy-start | bytes 6291460
  630.4 9.1 %copy-start.18 = (f32[4,1024,64]{1,2,0:T(8,128)S(1)}, f32[4,1024,64]{1,2,0:T(8,128)}, u32[]{:S(2)}) copy-start(f32[4,1024,64]{1,2,0:T(8,128)} %get-tuple-element.114) | copy-start | bytes 3145732
  630.4 9.1 %copy-start.19 = (f32[4,1024,64]{1,2,0:T(8,128)S(1)}, f32[4,1024,64]{1,2,0:T(8,128)}, u32[]{:S(2)}) copy-start(f32[4,1024,64]{1,2,0:T(8,128)} %get-tuple-element.113) | copy-start | bytes 3145732
  630.4 9.1 %copy-start.20 = (f32[4,1024,64]{1,2,0:T(8,128)S(1)}, f32[4,1024,64]{1,2,0:T(8,128)}, u32[]{:S(2)}) copy-start(f32[4,1024,64]{1,2,0:T(8,128)} %get-tuple-element.112) | copy-start | bytes 3145732
  630.4 9.1 %copy-start.21 = (f32[4,1024,64]{1,2,0:T(8,128)S(1)}, f32[4,1024,64]{1,2,0:T(8,128)}, u32[]{:S(2)}) copy-start(f32[4,1024,64]{1,2,0:T(8,128)} %get-tuple-element.111) | copy-start | bytes 3145732
  630.4 9.1 %copy-start.35 = (f32[1024,1,512]{2,0,1:T(8,128)S(1)}, f32[1024,1,512]{2,0,1:T(8,128)}, u32[]{:S(2)}) copy-start(f32[1024,1,512]{2,0,1:T(8,128)} %all-gather.5.cloned.1.call-done) | copy-start | bytes 6291460
  809.7 8.6 %copy-start.17 = (f32[512,1024]{1,0:T(8,128)S(1)}, f32[512,1024]{1,0:T(8,128)}, u32[]{:S(2)}) copy-start(f32[512,1024]{1,0:T(8,128)} %get-tuple-element.471) | copy-start | bytes 6291460
  (26 other events, 88.1 us)
Sparse Core Ops, SparseCore 0:
  15.3 35.8 all-gather.4
  155.2 31.8 reduce-scatter.4
  191.1 33.1 all-gather.6
  225.8 33.1 all-gather.8
  282.0 31.8 reduce-scatter.8
  316.0 31.8 reduce-scatter.6
  353.3 33.1 all-gather.10
  620.5 31.8 reduce-scatter.10
  658.7 150.9 all-reduce.2
where the time goes:
time: 837 us; the launch traced here: 828 us
  matrix products  362 us (43%)
  waiting for transfers between devices  307 us (37%)
  local copies, waits for them, and re-layouts  50.7 us (6%)
  blocking collectives  41.3 us (5%)
  loops' own time  31 us (4%)
  other arithmetic  21.5 us (3%)
  between operations  14.5 us (2%)
    dot_general x80, matrix products, product(): jnp.dot(left, right, precision=precise, preferred_element_type=jnp.float32)  326 us
    psum x1, waiting for transfers between devices, per_device(): lax.psum((grad_query, grad_key, grad_value, grad_control, grad_output, gr...  100 us
    psum x1, blocking collectives, per_device(): gain_stack = lax.psum(gain_stack, ('dp', 'head'))  41.3 us
    dot_general x4, matrix products, outer_sum(): jnp.einsum('rsi,rsj->ij', left, right, precision=precise, preferred_eleme...  35.3 us
    all_gather x1, waiting for transfers between devices, per_device(): row_piece = lax.all_gather(d_hidden, 'head', axis=0, tiled=True)  33.2 us
    all_gather x1, waiting for transfers between devices, per_device(): row_piece = lax.all_gather(second, 'head', axis=0, tiled=True)  32.6 us
    reduce_scatter x1, waiting for transfers between devices, per_device(): lax.psum_scatter(product(activated, down_weight), 'head', scatter_dimensi...  32.3 us
    reduce_scatter x1, waiting for transfers between devices, per_device(): lax.psum_scatter(product(attended, output_weight), 'head', scatter_dimens...  31.9 us
  transfers between devices with their start and end apart: 9, of which 8 were waited for; matrix products, arithmetic and copies ran while one was open for 9% of the time, Pallas kernels for 0%

commit v1 on v0

v1 whole, which is shorter than its diff:
```python
import jax
import jax.numpy as jnp
from jax import lax
from jax.experimental import pallas as pl
from jax.experimental.pallas import tpu as pltpu
from jax.sharding import PartitionSpec as P

F32 = jnp.float32
HIGH = lax.Precision.HIGH
CHUNK = 256
EPS = 1e-05
GELU_C = 0.7978845608028654
GELU_K = 0.044715
VMEM_LIMIT = 40 * 2**20


def dot(left, right, dims):
    return lax.dot_general(
        left, right, (dims, ((), ())), precision=HIGH, preferred_element_type=F32
    )


def nn(left, right):
    return dot(left, right, ((1,), (0,)))


def nt(left, right):
    return dot(left, right, ((1,), (1,)))


def tn(left, right):
    return dot(left, right, ((0,), (0,)))


def whole():
    return pl.BlockSpec(memory_space=pltpu.VMEM)


def scalars():
    return pl.BlockSpec(memory_space=pltpu.SMEM)


def cost(flops, arrays_in, arrays_out):
    size = sum(a.size * 4 for a in arrays_in) + sum(a.size * 4 for a in arrays_out)
    return pl.CostEstimate(flops=int(flops), bytes_accessed=int(size), transcendentals=0)


def run(kernel, outs, scal, arrays, flops, scratch=()):
    out_shape = [jax.ShapeDtypeStruct(shape, F32) for shape in outs]
    return pl.pallas_call(
        kernel,
        out_shape=out_shape,
        in_specs=[scalars()] * len(scal) + [whole()] * len(arrays),
        out_specs=[whole()] * len(outs),
        scratch_shapes=list(scratch),
        compiler_params=pltpu.CompilerParams(vmem_limit_bytes=VMEM_LIMIT),
        cost_estimate=cost(3 * flops, arrays, out_shape),
    )(*scal, *arrays)


def lane_slice(ref, index, width):
    return ref[:, pl.ds(pl.multiple_of(index * width, width), width)]


def normalize(x):
    centre = x - jnp.mean(x, axis=-1, keepdims=True)
    spread = jnp.mean(centre * centre, axis=-1, keepdims=True)
    r = lax.rsqrt(spread + EPS)
    return centre * r, r


def norm_back(dy, nhat, r, gain):
    dyg = dy * gain
    first = jnp.mean(dyg, axis=-1, keepdims=True)
    second = jnp.mean(dyg * nhat, axis=-1, keepdims=True)
    return r * (dyg - first - nhat * second)


def doc_of(starts, position):
    total = jnp.zeros(jnp.shape(position), jnp.int32)
    for k in range(starts.shape[1]):
        total = total + (position >= starts[0, k]).astype(jnp.int32)
    return total


def column(first, count):
    return first + lax.broadcasted_iota(jnp.int32, (count, 1), 0)


def left_lanes():
    return lax.broadcasted_iota(jnp.int32, (1, 128), 1) < 64


def pack_state(mk, mv, z):
    left = left_lanes()
    return jnp.concatenate(
        [
            jnp.where(left, mk[0:64], mk[64:128]),
            jnp.where(left, mv[0:64], mv[64:128]),
            jnp.broadcast_to(z, (8, 128)),
        ],
        axis=0,
    )


def blocks_only(m):
    diagonal = (lax.broadcasted_iota(jnp.int32, (128, 128), 0) < 64) == (
        lax.broadcasted_iota(jnp.int32, (128, 128), 1) < 64
    )
    return jnp.where(diagonal, m, 0.0)


def unpack_state(state):
    mk = state[0:64]
    mv = state[64:128]
    return (
        blocks_only(jnp.concatenate([mk, mk], axis=0)),
        blocks_only(jnp.concatenate([mv, mv], axis=0)),
        state[128:129],
    )


def end_state(k2, v2, e2, starts, first):
    count = k2.shape[0]
    kept = (doc_of(starts, column(first, count)) == doc_of(starts, first + count - 1)).astype(F32)
    em = e2 * kept
    return pack_state(tn(k2, em), tn(em, v2), jnp.sum(em, axis=0, keepdims=True))


def own_kernel(scal, starts, x, gain, shift, wq, wk, wv, wc, normed, proj, states):
    nhat, _ = normalize(x[...])
    n = nhat * gain[...] + shift[...]
    normed[...] = n
    for w, ref in enumerate((wq, wk, wv, wc)):
        full = nn(n, ref[...])
        if w == 3:
            full = jnp.exp(full)
        for p in range(2):
            proj[p, :, w * 128 : (w + 1) * 128] = full[:, p * 128 : (p + 1) * 128]
    for p in range(2):
        states[p] = end_state(
            proj[p, :, 128:256], proj[p, :, 256:384], proj[p, :, 384:512], starts, scal[0]
        )


def other_kernel(scal, starts, normed, wa, wb, proj, state):
    core = scal[1]
    full = nn(lane_slice(normed, core, 256), wa[...]) + nn(
        lane_slice(normed, 1 - core, 256), wb[...]
    )
    proj[:, 0:384] = full[:, 0:384]
    proj[:, 384:512] = jnp.exp(full[:, 384:512])
    state[...] = end_state(
        proj[:, 128:256], proj[:, 256:384], proj[:, 384:512], starts, scal[0]
    )


def chunk_masks(starts, first, c):
    begin = first + c * CHUNK
    position = column(begin, CHUNK)
    docs = doc_of(starts, position)
    row = begin + lax.broadcasted_iota(jnp.int32, (1, CHUNK), 1)
    mask = (position >= row) & (docs == doc_of(starts, row))
    before = doc_of(starts, begin - 1)
    last = doc_of(starts, begin + CHUNK - 1)
    entering = (docs == before).astype(F32)
    leaving = (docs == last).astype(F32)
    passing = (before == last).astype(F32)
    return mask, entering, leaving, passing


def halves(x):
    left = left_lanes()
    return jnp.where(left, x, 0.0), jnp.where(left, 0.0, x)


def per_head(x):
    left = left_lanes()
    return left, x


def attention_kernel(index, starts, proj, carry, o, saved):
    left = left_lanes()
    mk, mv, z_in = unpack_state(carry[0])
    for c in range(proj.shape[1] // CHUNK):
        rows = slice(c * CHUNK, (c + 1) * CHUNK)
        q2, k2 = proj[0, rows, 0:128], proj[0, rows, 128:256]
        v2, e2 = proj[0, rows, 256:384], proj[0, rows, 384:512]
        mask, entering, leaving, passing = chunk_masks(starts, index[2], c)
        z = nn(mask.astype(F32), e2) + entering * z_in
        total = entering * nn(q2, mk)
        parts = [nn(jnp.where(mask, nt(qh, k2), 0.0), e2) for qh in halves(q2)]
        total = total + jnp.where(left, parts[0], parts[1])
        s = total / z * 0.125
        top = jnp.where(
            left,
            jnp.max(jnp.where(left, s, -jnp.inf), axis=1, keepdims=True),
            jnp.max(jnp.where(left, -jnp.inf, s), axis=1, keepdims=True),
        )
        p = jnp.exp(s - top)
        pa, pb = halves(p)
        p = p / jnp.where(
            left, jnp.sum(pa, axis=1, keepdims=True), jnp.sum(pb, axis=1, keepdims=True)
        )
        r = p / z
        parts = [nn(jnp.where(mask, nt(rh, e2), 0.0), v2) for rh in halves(r)]
        o[rows, :] = jnp.where(left, parts[0], parts[1]) + entering * nn(r, mv)
        saved[rows, 0:128] = z
        saved[rows, 128:256] = s
        saved[rows, 256:384] = p
        if (c + 1) * CHUNK < proj.shape[1]:
            em = e2 * leaving
            mk = blocks_only(tn(k2, em)) + passing * mk
            mv = blocks_only(tn(em, v2)) + passing * mv
            z_in = jnp.sum(em, axis=0, keepdims=True) + passing * z_in


def attention_back_kernel(index, starts, proj, carry, saved, d_o, dproj, dstate):
    left = left_lanes()
    chunks = proj.shape[1] // CHUNK
    states = [unpack_state(carry[0])]
    for c in range(chunks - 1):
        rows = slice(c * CHUNK, (c + 1) * CHUNK)
        k2, v2, e2 = proj[0, rows, 128:256], proj[0, rows, 256:384], proj[0, rows, 384:512]
        _, _, leaving, passing = chunk_masks(starts, index[2], c)
        mk, mv, z_in = states[c]
        em = e2 * leaving
        states.append(
            (
                blocks_only(tn(k2, em)) + passing * mk,
                blocks_only(tn(em, v2)) + passing * mv,
                jnp.sum(em, axis=0, keepdims=True) + passing * z_in,
            )
        )
    ahead = None
    for c in reversed(range(chunks)):
        rows = slice(c * CHUNK, (c + 1) * CHUNK)
        q2, k2 = proj[0, rows, 0:128], proj[0, rows, 128:256]
        v2, e2 = proj[0, rows, 256:384], proj[0, rows, 384:512]
        z, s, p = saved[rows, 0:128], saved[rows, 128:256], saved[rows, 256:384]
        do2 = d_o[rows, :]
        mask, entering, leaving, passing = chunk_masks(starts, index[2], c)
        mk, mv, _ = states[c]
        r = p / z
        do_in = entering * do2
        parts_v, parts_r, parts_e = [], [], []
        for rh, doh in zip(halves(r), halves(do2)):
            mixing = jnp.where(mask, nt(rh, e2), 0.0)
            d_mixing = jnp.where(mask, nt(doh, v2), 0.0)
            parts_v.append(tn(mixing, do2))
            parts_r.append(nn(d_mixing, e2))
            parts_e.append(tn(d_mixing, r))
        dv = jnp.where(left, parts_v[0], parts_v[1])
        dr = jnp.where(left, parts_r[0], parts_r[1]) + nt(do_in, mv)
        de = jnp.where(left, parts_e[0], parts_e[1])
        dp = dr / z
        dz = -dp * r
        pdp = p * dp
        pa, pb = halves(pdp)
        inner = jnp.where(
            left, jnp.sum(pa, axis=1, keepdims=True), jnp.sum(pb, axis=1, keepdims=True)
        )
        ds = p * (dp - inner) / z
        w = ds * 0.125
        dz = dz - ds * s
        w_in = entering * w
        parts_q, parts_k, parts_e = [], [], []
        for qh, wh in zip(halves(q2), halves(w)):
            affinity = jnp.where(mask, nt(qh, k2), 0.0)
            d_affinity = jnp.where(mask, nt(wh, e2), 0.0)
            parts_q.append(nn(d_affinity, k2))
            parts_k.append(tn(d_affinity, q2))
            parts_e.append(tn(affinity, w))
        dq = jnp.where(left, parts_q[0], parts_q[1]) + nt(w_in, mk)
        dk = jnp.where(left, parts_k[0], parts_k[1])
        de = de + jnp.where(left, parts_e[0], parts_e[1]) + tn(mask.astype(F32), dz)
        if ahead is not None:
            dmk, dmv, dz_out = ahead
            em = e2 * leaving
            dv = dv + nn(em, dmv)
            dk = dk + nt(em, dmk)
            de = de + leaving * (nn(k2, dmk) + nt(v2, dmv) + dz_out)
        dproj[rows, 0:128] = dq
        dproj[rows, 128:256] = dk
        dproj[rows, 256:384] = dv
        dproj[rows, 384:512] = de
        now = (
            blocks_only(tn(q2, w_in)),
            blocks_only(tn(r, do_in)),
            jnp.sum(entering * dz, axis=0, keepdims=True),
        )
        if ahead is not None:
            now = tuple(a + passing * b for a, b in zip(now, ahead))
        ahead = now
    dstate[...] = pack_state(*ahead)


def qkvc_kernel(index, starts, proj, dstate, normed, dproj, send, keep, final):
    k2, v2, e2 = proj[0, :, 128:256], proj[0, :, 256:384], proj[0, :, 384:512]
    count = k2.shape[0]
    first = index[2]
    core = index[3]
    dmk, dmv, dz_out = unpack_state(dstate[...])
    leaving = (
        doc_of(starts, column(first, count)) == doc_of(starts, first + count - 1)
    ).astype(F32)
    em = e2 * leaving
    final[:, 0:128] = dproj[:, 0:128]
    final[:, 128:256] = dproj[:, 128:256] + nt(em, dmk)
    final[:, 256:384] = dproj[:, 256:384] + nn(em, dmv)
    de = dproj[:, 384:512] + leaving * (nn(k2, dmk) + nt(v2, dmv) + dz_out)
    final[:, 384:512] = e2 * de
    send[...] = tn(lane_slice(normed, 1 - core, 256), final[...])
    keep[...] = tn(lane_slice(normed, core, 256), final[...])


def pair_call(kernel, outs, index, starts, proj, carry, arrays, flops):
    out_shape = [jax.ShapeDtypeStruct(shape, F32) for shape in outs]

    def pick(which):
        return lambda i, index, starts: (index[which], 0, 0)

    def all_of(a):
        zeros = (0,) * len(a.shape)
        return pl.BlockSpec(a.shape, lambda i, index, starts: zeros)

    return pl.pallas_call(
        kernel,
        out_shape=out_shape,
        grid_spec=pltpu.PrefetchScalarGridSpec(
            num_scalar_prefetch=2,
            grid=(1,),
            in_specs=[
                pl.BlockSpec((1,) + proj.shape[1:], pick(0)),
                pl.BlockSpec((1,) + carry.shape[1:], pick(1)),
            ]
            + [all_of(a) for a in arrays],
            out_specs=[all_of(a) for a in out_shape],
        ),
        compiler_params=pltpu.CompilerParams(vmem_limit_bytes=VMEM_LIMIT),
        cost_estimate=cost(3 * flops, (proj,) + tuple(arrays), out_shape),
    )(index, starts, proj, carry, *arrays)


def middle_kernel(scal, x, o0, o1, o2, o3, wo, wo2, wo3, gain, shift, hidden, second, o_all, w_all):
    pair = scal[2]
    for j, ref in enumerate((o0, o1, o2, o3)):
        o_all[:, j * 128 : (j + 1) * 128] = ref[...]
    for j in range(2):
        which = pair * (1 - 2 * j) + j
        w_all[j * 128 : (j + 1) * 128, :] = wo[pl.ds(pl.multiple_of(which * 128, 128), 128), :]
    w_all[256:384, :] = wo2[...]
    w_all[384:512, :] = wo3[...]
    h = x[...] + nn(o_all[...], w_all[...])
    hidden[...] = h
    nhat, _ = normalize(h)
    second[...] = nhat * gain[...] + shift[...]


def middle_back_kernel(
    scal, hidden, cot, ds0, ds1, ds2, ds3, u0, u1, u2, u3, gain, o_all, w_all,
    outputs, d_hidden, grads, d_o, send, keep, work,
):
    core = scal[1]
    outputs[...] = hidden[...] + ((u0[...] + u1[...]) + (u2[...] + u3[...]))
    d_second = (ds0[...] + ds1[...]) + (ds2[...] + ds3[...])
    nhat, r = normalize(hidden[...])
    grads[0:1, :] = jnp.sum(d_second * nhat, axis=0, keepdims=True)
    grads[1:2, :] = jnp.sum(d_second, axis=0, keepdims=True)
    grads[2:8, :] = jnp.zeros((6, grads.shape[1]), F32)
    d = cot[...] + norm_back(d_second, nhat, r, gain[...])
    d_hidden[...] = d
    d_o[...] = nt(d, w_all[...])
    work[...] = tn(o_all[...], d)
    for ref, which in ((send, 1 - core), (keep, core)):
        for j in range(4):
            rows = pl.ds(pl.multiple_of(j * 128 + which * 64, 64), 64)
            for b in range(4):
                ref[j, b * 64 : (b + 1) * 64, :] = work[rows, b * 128 : (b + 1) * 128]


def ff_kernel(refs_in, second, cot, blocks, received, outs):
    d_second = None
    for half, (up, down) in enumerate(blocks):
        u = nn(second[...], up[...])
        inner = GELU_C * (u + GELU_K * u * u * u)
        t = jnp.tanh(inner)
        act = 0.5 * u * (1.0 + t)
        slope = 0.5 * (1.0 + t) + 0.5 * u * (1.0 - t * t) * (
            GELU_C * (1.0 + 3.0 * GELU_K * u * u)
        )
        du = nt(cot[...], down[...]) * slope
        g_up = tn(second[...], du)
        g_down = tn(act, cot[...])
        if received is not None:
            g_up = g_up + received[half][...]
            g_down = g_down + received[2 + half][...]
        outs[half][...] = g_up
        outs[2 + half][...] = g_down
        if half == 0:
            outs[4][...] = nn(act, down[...])
            outs[5][...] = nt(du, up[...])
        else:
            outs[4][...] = outs[4][...] + nn(act, down[...])
            outs[5][...] = outs[5][...] + nt(du, up[...])


def ff_call(which, second, cot, up_own, down_own, up_oth, down_oth, received):
    rows, width = second.shape
    block = up_oth.shape[1]
    shapes = [(width, block)] * 2 + [(block, width)] * 2 + [(rows, width)] * 2
    out_shape = [jax.ShapeDtypeStruct(shape, F32) for shape in shapes]

    def kernel(index, second, cot, u_own, d_own, u_oth, d_oth, *rest):
        count = 0 if received is None else 4
        ff_kernel(
            None, second, cot, ((u_own, d_own), (u_oth, d_oth)),
            rest[:4] if count else None, rest[count:],
        )

    def all_of(a):
        zeros = (0,) * len(a.shape)
        return pl.BlockSpec(a.shape, lambda i, index: zeros)

    extra = () if received is None else tuple(received)
    arrays = (second, cot, up_own, down_own, up_oth, down_oth) + extra
    return pl.pallas_call(
        kernel,
        out_shape=out_shape,
        grid_spec=pltpu.PrefetchScalarGridSpec(
            num_scalar_prefetch=1,
            grid=(1,),
            in_specs=[
                all_of(second),
                all_of(cot),
                pl.BlockSpec((width, block), lambda i, index: (0, index[0])),
                pl.BlockSpec((block, width), lambda i, index: (index[0], 0)),
                all_of(up_oth),
                all_of(down_oth),
            ]
            + [all_of(a) for a in extra],
            out_specs=[all_of(a) for a in out_shape],
        ),
        compiler_params=pltpu.CompilerParams(vmem_limit_bytes=VMEM_LIMIT),
        cost_estimate=cost(3 * 2 * 6 * rows * width * 2 * block, (second, cot) + extra, out_shape),
    )(which, *arrays)


def first_back_kernel(
    scal, x, gain, d_hidden, f0, f1, f2, f3, wq, wk, wv, wc, a0, b0, a1, b1,
    grad_x, grads, cat, acc,
):
    core, pair = scal[1], scal[2]
    for j, ref in enumerate((f0, f1)):
        which = pair * (1 - 2 * j) + j
        for w in range(4):
            start = pl.multiple_of(w * 256 + which * 128, 128)
            cat[:, pl.ds(start, 128)] = ref[:, w * 128 : (w + 1) * 128]
    total = nt(cat[:, 0:256], wq[...])
    for w, ref in ((1, wk), (2, wv), (3, wc)):
        total = total + nt(cat[:, w * 256 : (w + 1) * 256], ref[...])
    acc[...] = total
    for which, refs in ((core, (a0, a1)), (1 - core, (b0, b1))):
        part = nt(f2[...], refs[0][...]) + nt(f3[...], refs[1][...])
        lanes = pl.ds(pl.multiple_of(which * 256, 256), 256)
        acc[:, lanes] = acc[:, lanes] + part
    d_normed = acc[...]
    nhat, r = normalize(x[...])
    grads[0:1, :] = jnp.sum(d_normed * nhat, axis=0, keepdims=True)
    grads[1:2, :] = jnp.sum(d_normed, axis=0, keepdims=True)
    grads[2:8, :] = jnp.zeros((6, grads.shape[1]), F32)
    grad_x[...] = d_hidden[...] + norm_back(d_normed, nhat, r, gain[...])


def combine(groups, radix, index):
    flat = [a for group in groups for a in group]
    counts = [len(group) for group in groups]
    shapes = []
    for group in groups:
        rows, cols = group[0].shape
        shapes += [(rows // radix, cols)] * radix

    def kernel(idx, *refs):
        ins, outs = refs[: len(flat)], refs[len(flat) :]
        at = 0
        for g, count in enumerate(counts):
            terms = ins[at : at + count]
            at += count
            rows = terms[0].shape[0] // radix
            for k in range(radix):
                if radix == 1:
                    value = terms[0][...]
                    for term in terms[1:]:
                        value = value + term[...]
                else:
                    where = jnp.bitwise_xor(idx[0], k)
                    block = pl.ds(pl.multiple_of(where * rows, rows), rows)
                    value = terms[0][block, :]
                    for term in terms[1:]:
                        value = value + term[block, :]
                outs[g * radix + k][...] = value

    outs = run(kernel, shapes, (index,), flat, 0)
    return [outs[g * radix : (g + 1) * radix] for g in range(len(groups))]


def assemble(groups, index):
    flat = [a for group in groups for a in group]
    radix = len(groups[0])
    shapes = [(group[0].shape[0] * radix, group[0].shape[1]) for group in groups]

    def kernel(idx, *refs):
        ins, outs = refs[: len(flat)], refs[len(flat) :]
        for g in range(len(groups)):
            for k in range(radix):
                piece = ins[g * radix + k]
                rows = piece.shape[0]
                where = jnp.bitwise_xor(idx[0], k)
                outs[g][pl.ds(pl.multiple_of(where * rows, rows), rows), :] = piece[...]

    return run(kernel, shapes, (index,), flat, 0)


def up_assemble_kernel(idx, u0, u1, u2, u3, d0, d1, d2, d3, up, down):
    width = u0.shape[1]
    for k, (u, d) in enumerate(((u0, d0), (u1, d1), (u2, d2), (u3, d3))):
        where = pl.ds(pl.multiple_of(jnp.bitwise_xor(idx[3], k) * width, width), width)
        up[:, where] = u[...]
        down[where, :] = d[...]


def qkvc_assemble_kernel(idx, g0, g1, g2, g3, o0, o1, o2, o3, wq, wk, wv, wc, wo):
    core, pair = idx[1], idx[2]
    for j in range(4):
        g = (g0, g1, g2, g3)[j]
        o = (o0, o1, o2, o3)[j]
        half = core if j % 2 == 0 else 1 - core
        which = pair if j < 2 else 1 - pair
        rows = pl.ds(pl.multiple_of(half * 256, 256), 256)
        lanes = pl.ds(pl.multiple_of(which * 128, 128), 128)
        for w, ref in enumerate((wq, wk, wv, wc)):
            ref[rows, lanes] = g[:, w * 128 : (w + 1) * 128]
        out_rows = pl.ds(pl.multiple_of(which * 128 + half * 64, 64), 64)
        for b in range(4):
            wo[out_rows, b * 128 : (b + 1) * 128] = o[b * 64 : (b + 1) * 64, :]


def per_device(
    inputs, doc_starts, query_weight, key_weight, value_weight, control_weight, output_weight,
    up_weight, down_weight, first_gain, first_shift, second_gain, second_shift, cotangent,
):
    rows, _, width = inputs.shape
    x = inputs.reshape(rows, width)
    cot = cotangent.reshape(rows, width)
    devices = lax.axis_size("dp")
    place = lax.axis_index("dp").astype(jnp.int32)
    y = lax.axis_index("head").astype(jnp.int32)
    core = place & 1
    pair = (place >> 1) & 1
    rank = place & 3
    first = y * rows
    one = lambda *v: jnp.stack([jnp.asarray(a, jnp.int32) for a in v])
    scal = one(first, core, pair, rank)
    gain1, shift1 = first_gain.reshape(1, width), first_shift.reshape(1, width)
    gain2, shift2 = second_gain.reshape(1, width), second_shift.reshape(1, width)

    def swap_y(a):
        return lax.ppermute(a, "head", [(0, 1), (1, 0)])

    def swap(a, bits):
        return lax.ppermute(a, "dp", [(i, i ^ bits) for i in range(devices)])

    weights = (query_weight, key_weight, value_weight, control_weight)
    piece = jnp.concatenate(
        [lax.dynamic_slice(w, (core * 256, pair * 128), (256, 128)) for w in weights], axis=1
    )
    wo_piece = lax.dynamic_slice(output_weight, (pair * 128 + core * 64, 0), (64, width))
    block = up_weight.shape[1] // 4
    up_piece = lax.dynamic_slice(up_weight, (0, rank * block), (width, block))
    down_piece = lax.dynamic_slice(down_weight, (rank * block, 0), (block, width))
    qa0 = swap_y(piece)
    wo0 = swap_y(wo_piece)
    up0 = swap_y(up_piece)
    down0 = swap_y(down_piece)
    qb0 = swap(qa0, 1)
    qa1 = swap(qa0, 2)
    qb1 = swap(qa1, 1)
    wo1 = swap(wo0, 2)
    wo0b, wo1b = swap(wo0, 1), swap(wo1, 1)
    up2, down2 = swap(up0, 2), swap(down0, 2)
    up1, down1 = swap(up0, 1), swap(down0, 1)
    up3, down3 = swap(up2, 1), swap(down2, 1)
    even = core == 0
    wo_pair0 = jnp.where(even, jnp.concatenate([wo0, wo0b]), jnp.concatenate([wo0b, wo0]))
    wo_pair1 = jnp.where(even, jnp.concatenate([wo1, wo1b]), jnp.concatenate([wo1b, wo1]))

    normed, proj_own, states_own = run(
        own_kernel,
        [(rows, width), (2, rows, 512), (2, 136, 128)],
        (scal, doc_starts),
        (x, gain1, shift1) + weights,
        2 * rows * width * 1024,
    )
    proj_oth, states_oth = [], []
    for wa, wb in ((qa0, qb0), (qa1, qb1)):
        got = run(
            other_kernel,
            [(rows, 512), (136, 128)],
            (scal, doc_starts),
            (normed, wa, wb),
            2 * rows * width * 512,
        )
        proj_oth.append(got[0][None])
        states_oth.append(got[1])
    to_second = lambda a: lax.ppermute(a, "head", [(0, 1)])
    to_first = lambda a: lax.ppermute(a, "head", [(1, 0)])
    carry_oth = to_second(states_own)
    carry_own = [to_second(s)[None] for s in states_oth]

    zero = jnp.int32(0)
    setups = []
    for j in range(2):
        setups.append((one(pair ^ j, zero, first, core), proj_own, carry_own[j]))
    for j in range(2):
        setups.append((one(zero, pair ^ j, first, core), proj_oth[j], carry_oth))
    attn_flops = 2 * rows * CHUNK * 128
    fwd = {}
    for j in (2, 0, 3, 1):
        index, proj, carry = setups[j]
        fwd[j] = pair_call(
            attention_kernel, [(rows, 128), (rows, 384)], index, doc_starts, proj, carry, (),
            13 * attn_flops,
        )
    hidden, second, o_all, w_all = run(
        middle_kernel,
        [(rows, width)] * 2 + [(rows, 512), (512, width)],
        (scal,),
        (x,) + tuple(fwd[j][0] for j in range(4))
        + (output_weight, wo_pair0, wo_pair1, gain2, shift2),
        2 * rows * width * 512,
    )

    ups, downs = (up0, up1, up2, up3), (down0, down1, down2, down3)

    def ff(j, received):
        return ff_call(
            one(rank ^ j), second, cot, up_weight, down_weight, ups[j], downs[j], received
        )

    ff3 = ff(3, None)
    sent3 = [swap(a, 1) for a in ff3[:4]]
    ff1 = ff(1, None)
    sent1 = [swap(a, 1) for a in ff1[:4]]
    ff2 = ff(2, sent3)
    ff0 = ff(0, sent1)

    rest = devices // 4
    stages = []
    shift = 2
    while rest > 1:
        radix = 4 if rest % 4 == 0 and rest != 8 else rest
        stages.append((shift, radix))
        shift += radix.bit_length() - 1
        rest //= radix

    def reduce_chunk(own0, oth0, own1, oth1):
        got1 = [swap_y(a) for a in oth1]
        sum1 = [g[0] for g in combine([[a, b] for a, b in zip(own1, got1)], 1, one(zero))]
        got_x = [swap(a, 2) for a in sum1]
        got0 = [swap_y(a) for a in oth0]
        groups = [[a, b, c] for a, b, c in zip(own0, got0, got_x)]
        for at, radix in stages:
            where = (place >> at) & (radix - 1)
            pieces = combine(groups, radix, one(where))
            groups = [
                [group[0]] + [swap(group[m], m << at) for m in range(1, radix)]
                for group in pieces
            ]
        shards = [g[0] for g in combine(groups, 1, one(zero))]
        for at, radix in reversed(stages):
            where = (place >> at) & (radix - 1)
            shards = assemble(
                [[a] + [swap(a, m << at) for m in range(1, radix)] for a in shards], one(where)
            )
        far = [swap(a, 2) for a in shards]
        near_all = [swap(a, 1) for a in shards]
        far_all = [swap(a, 1) for a in far]
        return [list(v) for v in zip(shards, near_all, far, far_all)]

    ff_sums = reduce_chunk(
        [ff0[0], ff0[2]], [ff0[1], ff0[3]], [ff2[0], ff2[2]], [ff2[1], ff2[3]]
    )
    grad_up, grad_down = run(
        up_assemble_kernel,
        [up_weight.shape, down_weight.shape],
        (scal,),
        tuple(ff_sums[0]) + tuple(ff_sums[1]),
        0,
    )

    outputs, d_hidden, grads2, d_o, o_send, o_keep = run(
        middle_back_kernel,
        [(rows, width)] * 2 + [(8, width), (rows, 512), (4, 256, 128), (4, 256, 128)],
        (scal,),
        (hidden, cot, ff0[5], ff1[5], ff2[5], ff3[5], ff0[4], ff1[4], ff2[4], ff3[4], gain2, o_all, w_all),
        4 * rows * width * 512,
        (pltpu.VMEM((512, width), F32),),
    )
    o_got = swap(o_send, 1)

    back = {}
    for j in (1, 3, 0, 2):
        index, proj, carry = setups[j]
        back[j] = pair_call(
            attention_back_kernel, [(rows, 512), (136, 128)], index, doc_starts, proj, carry,
            (fwd[j][1], d_o[:, j * 128 : (j + 1) * 128]), 28 * attn_flops,
        )
    grads = {}
    for j in (1, 3, 0, 2):
        index, proj, _ = setups[j]
        dstate = to_first(back[(j + 2) % 4][1])

        def kernel(idx, starts, proj, dst, normed, dproj, send, keep, final):
            qkvc_kernel(idx, starts, proj, dst.at[0], normed, dproj, send, keep, final)

        index = index.at[1].set(0)
        grads[j] = pair_call(
            kernel, [(256, 512), (256, 512), (rows, 512)], index, doc_starts, proj, dstate[None],
            (normed, back[j][0]), 2 * rows * width * 512,
        )
    summed = {}
    for j in (1, 3, 0, 2):
        got = swap(grads[j][0], 1)
        parts = combine([[grads[j][1], got], [o_keep[j], o_got[j]]], 1, one(zero))
        summed[j] = [p[0] for p in parts]
    sums = reduce_chunk(summed[0], summed[2], summed[1], summed[3])
    grad_query, grad_key, grad_value, grad_control, grad_output = run(
        qkvc_assemble_kernel,
        [w.shape for w in weights] + [output_weight.shape],
        (scal,),
        tuple(sums[0]) + tuple(sums[1]),
        0,
    )

    grad_inputs, grads1 = run(
        first_back_kernel,
        [(rows, width), (8, width)],
        (scal,),
        (x, gain1, d_hidden, grads[0][2], grads[1][2], grads[2][2], grads[3][2]) + weights
        + (qa0, qb0, qa1, qb1),
        2 * rows * width * 2048,
        (pltpu.VMEM((rows, 1024), F32), pltpu.VMEM((rows, width), F32)),
    )
    gains = jnp.concatenate([grads1[0:2], grads2[0:2]], axis=0)
    gains = gains + swap_y(gains)
    gains = gains + swap(gains, 1)
    gains = gains + swap(gains, 2)
    for at, radix in stages:
        gains = gains + sum(swap(gains, m << at) for m in range(1, radix))
    return (
        outputs.reshape(rows, 1, width), grad_inputs.reshape(rows, 1, width),
        grad_query, grad_key, grad_value, grad_control, grad_output, grad_up, grad_down,
        gains[0], gains[1], gains[2], gains[3],
    )


def solution(mesh):
    rows = P("head", "dp", None)
    cols = P(None, "head")
    tall = P("head", None)
    flat = P()
    return jax.shard_map(
        per_device,
        mesh=mesh,
        in_specs=(
            rows, P("dp", None), cols, cols, cols, cols, tall, cols, tall,
            flat, flat, flat, flat, rows,
        ),
        out_specs=(
            rows, rows, cols, cols, cols, cols, tall, cols, tall, flat, flat, flat, flat,
        ),
        check_vma=False,
    )
```

time: 837 us -> 415 us (0.50)
  matrix products: 362 us -> 0 us
  waiting for transfers between devices: 307 us -> 112 us
  Pallas kernels: 0 us -> 120 us
  starting transfers between devices: 0.37 us -> 105 us
  blocking collectives: 41.3 us -> 0 us
  loops' own time: 31 us -> 0 us
  other arithmetic: 21.5 us -> 1.53 us
  local copies, waits for them, and re-layouts: 50.7 us -> 68.7 us
  between operations: 14.5 us -> 2.07 us
    dot_general x84 -> x0, matrix products: 362 us -> none  [the longest x80 326 us: product(): jnp.dot(left, right, precision=precise, preferred_element_type=jnp.float32)]
    all_gather x4 -> x0, waiting for transfers between devices: 121 us -> none  [the longest x1 33.2 us: per_device(): row_piece = lax.all_gather(d_hidden, 'head', axis=0, tiled=True)]
    pallas_call x0 -> x36, Pallas kernels: none -> 120 us  [the longest x12 55.9 us: pair_call(): pl.pallas_call(kernel, out_shape=out_shape, grid_spec=pltpu.PrefetchScala...]
    ppermute x0 -> x90, waiting for transfers between devices: none -> 112 us  [the longest x70 77.2 us: swap(): return lax.ppermute(a, 'dp', [(i, i ^ bits) for i in range(devices)])]
    ppermute x0 -> x90, starting transfers between devices: none -> 105 us  [the longest x70 75 us: swap(): return lax.ppermute(a, 'dp', [(i, i ^ bits) for i in range(devices)])]
    psum x1 -> x0, waiting for transfers between devices: 100 us -> none  [per_device(): lax.psum((grad_query, grad_key, grad_value, grad_control, grad_output, gr...]
    reduce_scatter x4 -> x0, waiting for transfers between devices: 84.6 us -> none  [the longest x1 32.3 us: per_device(): lax.psum_scatter(product(activated, down_weight), 'head', scatter_dimensi...]
    psum x1 -> x0, blocking collectives: 41.3 us -> none  [per_device(): gain_stack = lax.psum(gain_stack, ('dp', 'head'))]
  transfers between devices with their start and end apart: 9 -> 90, of which waited for: 8 -> 23; matrix products, arithmetic and copies ran while one was open for 9% -> 4% of each run, Pallas kernels for 0% -> 29%
where the time goes in v1:
time: 415 us; the launch traced here: 409 us
  Pallas kernels  120 us (29%)
  waiting for transfers between devices  112 us (27%)
  starting transfers between devices  105 us (25%)
  local copies, waits for them, and re-layouts  68.7 us (17%)
    ppermute x70, waiting for transfers between devices, swap(): return lax.ppermute(a, 'dp', [(i, i ^ bits) for i in range(devices)])  77.2 us
    ppermute x70, starting transfers between devices, swap(): return lax.ppermute(a, 'dp', [(i, i ^ bits) for i in range(devices)])  75 us
    unnamed x214, local copies, waits for them, and re-layouts  57.4 us
    pallas_call x12, Pallas kernels, pair_call(): pl.pallas_call(kernel, out_shape=out_shape, grid_spec=pltpu.PrefetchScala...  55.9 us
    pallas_call x20, Pallas kernels, run(): pl.pallas_call(kernel, out_shape=out_shape, in_specs=[scalars()] * len(sc...  34.2 us
    ppermute x13, waiting for transfers between devices, swap_y(): return lax.ppermute(a, 'head', [(0, 1), (1, 0)])  30.3 us
    pallas_call x4, Pallas kernels, ff_call(): pl.pallas_call(kernel, out_shape=out_shape, grid_spec=pltpu.PrefetchScala...  29.9 us
    ppermute x13, starting transfers between devices, swap_y(): return lax.ppermute(a, 'head', [(0, 1), (1, 0)])  12.2 us
  transfers between devices with their start and end apart: 90, of which 23 were waited for; matrix products, arithmetic and copies ran while one was open for 4% of the time, Pallas kernels for 29%

profile of v1, /device:TPU:0, one launch (start us, length us, event | category | flops | bytes accessed | tf_op | source)
XLA Modules:
  0.0 409.3 jit_solution(4767936348941138354)
XLA Ops:
  14.3 6.0 %collective-permute-done.wa.a0 = f32[256,512]{1,0:T(8,128)} collective-permute-done((f32[256,512]{1,0:T(8,128)S(1)}, f32[256,512]{1,0:T(8,128)}, u32[]{:S(2)}, u32[]{:S(2)}) %collective-permute-start) | collective-permute-done | bytes 524320 | tf_op jit(solution)/shard_map/ppermute | solution.py:568
  22.6 22.2 %collective-permute-done.7 = f32[64,512]{1,0:T(8,128)S(1)} collective-permute-done((f32[64,512]{1,0:T(8,128)S(1)}, f32[64,512]{1,0:T(8,128)S(1)}, u32[]{:S(2)}, u32[]{:S(2)}) %collective-permute-start.7) | collective-permute-done | bytes 131104 | tf_op jit(solution)/shard_map/ppermute | solution.py:568
  66.7 3.9 collective-permute-start.2
  70.8 9.3 %collective-permute-done.19.u_oth = f32[512,256]{1,0:T(8,128)} collective-permute-done((f32[512,256]{1,0:T(8,128)}, f32[512,256]{1,0:T(8,128)}, u32[]{:S(2)}, u32[]{:S(2)}) %collective-permute-start.19) | collective-permute-done | bytes 524320 | tf_op jit(solution)/shard_map/ppermute | solution.py:571
  80.1 4.2 %shard_map.242 = (f32[512,128]{1,0:T(8,128)S(1)}, f32[512,384]{1,0:T(8,128)S(1)}) custom-call(s32[4]{0:T(128)S(1)} %get-tuple-element.318.index, s32[1,4]{1,0:T(1,128)S(1)} %copy-done.66, f32[1,512,512]{2,1,0:T(8,128)S(1)} %bitcast.57, f32[2,136,128]{2,1,0:T(8,128)S(1)} %collective-permute-done.6.carry), custom_call_target="tpu_custom_call" | custom-call | flops 1308622848 | bytes 2097152 | tf_op jit(solution)/shard_map/pallas_call | solution.py:327
  85.0 4.2 %shard_map.239 = (f32[512,128]{1,0:T(8,128)S(1)}, f32[512,384]{1,0:T(8,128)S(1)}) custom-call(s32[4]{0:T(128)S(1)} %fusion.5.index, s32[1,4]{1,0:T(1,128)S(1)} %copy-done.66, f32[2,512,512]{2,1,0:T(8,128)S(1)} %get-tuple-element.175.proj, f32[1,136,128]{2,1,0:T(8,128)S(1)} %bitcast.72), custom_call_target="tpu_custom_call" | custom-call | flops 1308622848 | bytes 3145728 | tf_op jit(solution)/shard_map/pallas_call | solution.py:327
  92.1 4.0 collective-permute-start.5
  96.0 4.2 %shard_map.243 = (f32[512,128]{1,0:T(8,128)S(1)}, f32[512,384]{1,0:T(8,128)S(1)}) custom-call(s32[4]{0:T(128)S(1)} %get-tuple-element.319.index, s32[1,4]{1,0:T(1,128)S(1)} %copy-done.66, f32[1,512,512]{2,1,0:T(8,128)S(1)} %bitcast.60, f32[2,136,128]{2,1,0:T(8,128)S(1)} %collective-permute-done.6.carry), custom_call_target="tpu_custom_call" | custom-call | flops 1308622848 | bytes 2097152 | tf_op jit(solution)/shard_map/pallas_call | solution.py:327
  101.2 4.2 %shard_map.241 = (f32[512,128]{1,0:T(8,128)S(1)}, f32[512,384]{1,0:T(8,128)S(1)}) custom-call(s32[4]{0:T(128)S(1)} %fusion.7.index, s32[1,4]{1,0:T(1,128)S(1)} %copy-done.66, f32[2,512,512]{2,1,0:T(8,128)S(1)} %get-tuple-element.175.proj, f32[1,136,128]{2,1,0:T(8,128)S(1)} %bitcast.74), custom_call_target="tpu_custom_call" | custom-call | flops 1308622848 | bytes 3145728 | tf_op jit(solution)/shard_map/pallas_call | solution.py:327
  110.4 6.6 %shard_map.247 = (f32[512,256]{1,0:T(8,128)}, f32[512,256]{1,0:T(8,128)}, f32[256,512]{1,0:T(8,128)}, f32[256,512]{1,0:T(8,128)S(1)}, f32[512,512]{1,0:T(8,128)S(1)}, /*index=5*/f32[512,512]{1,0:T(8,128)S(1)}) custom-call(s32[1]{0:T(128)} %bitcast.15.index, f32[512,512]{1,0:T(8,128)S(1)} %get-tuple-element.187.second, f32[512,512]{1,0:T(8,128)S(1)} %bitcast.52, ...), custom_call_target="tpu_custom_call" | custom-call | flops 4831838208 | bytes 6291456 | tf_op jit(solution)/shard_map/pallas_call | solution.py:427
  126.6 7.5 %shard_map.245 = (f32[512,256]{1,0:T(8,128)}, f32[512,256]{1,0:T(8,128)}, f32[256,512]{1,0:T(8,128)}, f32[256,512]{1,0:T(8,128)}, f32[512,512]{1,0:T(8,128)S(1)}, /*index=5*/f32[512,512]{1,0:T(8,128)S(1)}) custom-call(s32[1]{0:T(128)} %bitcast.13.index, f32[512,512]{1,0:T(8,128)S(1)} %copy-done.81, f32[512,512]{1,0:T(8,128)S(1)} %bitcast.53, ...), custom_call_target="tpu_custom_call" | custom-call | flops 4831838208 | bytes 6291456 | tf_op jit(solution)/shard_map/pallas_call | solution.py:427
  142.7 8.1 %shard_map.248 = (f32[512,256]{1,0:T(8,128)S(1)}, f32[512,256]{1,0:T(8,128)}, f32[256,512]{1,0:T(8,128)S(1)}, f32[256,512]{1,0:T(8,128)}, f32[512,512]{1,0:T(8,128)S(1)}, /*index=5*/f32[512,512]{1,0:T(8,128)S(1)}) custom-call(s32[1]{0:T(128)} %bitcast.14.index, f32[512,512]{1,0:T(8,128)S(1)} %copy-done.82, f32[512,512]{1,0:T(8,128)S(1)} %bitcast.54, ...), custom_call_target="tpu_custom_call" | custom-call | flops 4831838208 | bytes 8388608 | tf_op jit(solution)/shard_map/pallas_call | solution.py:427
  153.7 7.7 %shard_map.246 = (f32[512,256]{1,0:T(8,128)S(1)}, f32[512,256]{1,0:T(8,128)S(1)}, f32[256,512]{1,0:T(8,128)S(1)}, f32[256,512]{1,0:T(8,128)S(1)}, f32[512,512]{1,0:T(8,128)S(1)}, /*index=5*/f32[512,512]{1,0:T(8,128)S(1)}) custom-call(s32[1]{0:T(128)} %bitcast.3.index, f32[512,512]{1,0:T(8,128)S(1)} %copy-done.82, f32[512,512]{1,0:T(8,128)S(1)} %bitcast.55, ...), custom_call_target="tpu_custom_call" | custom-call | flops 4831838208 | bytes 8388608 | tf_op jit(solution)/shard_map/pallas_call | solution.py:427
  169.0 5.5 %shard_map.249 = (f32[512,512]{1,0:T(8,128)S(1)}, f32[512,512]{1,0:T(8,128)S(1)}, f32[8,512]{1,0:T(8,128)S(1)}, f32[512,512]{1,0:T(8,128)S(1)}, f32[4,256,128]{2,1,0:T(8,128)S(1)}, /*index=5*/f32[4,256,128]{2,1,0:T(8,128)S(1)}) custom-call(s32[4]{0:T(128)S(1)} %pad_add_fusion.4.scal.idx, f32[512,512]{1,0:T(8,128)S(1)} %copy-done.14, ...), custom_call_target="tpu_custom_call" | custom-call | flops 1610612736 | bytes 16795648 | tf_op jit(solution)/shard_map/pallas_call | solution.py:50
  177.3 7.3 %shard_map.253 = (f32[512,512]{1,0:T(8,128)S(1)}, f32[136,128]{1,0:T(8,128)S(1)}) custom-call(s32[4]{0:T(128)S(1)} %get-tuple-element.319.index, s32[1,4]{1,0:T(1,128)S(1)} %copy-done.66, f32[1,512,512]{2,1,0:T(8,128)S(1)} %bitcast.61, f32[2,136,128]{2,1,0:T(8,128)S(1)} %collective-permute-done.6.carry, f32[512,384]{1,0:T(8,128)S(1)} %copy-done.101, ...), custom_call_target="tpu_custom_call" | custom-call | flops 2818572288 | bytes 3215360 | tf_op jit(solution)/shard_map/pallas_call | solution.py:327
  186.1 7.2 %shard_map.254 = (f32[512,512]{1,0:T(8,128)S(1)}, f32[136,128]{1,0:T(8,128)S(1)}) custom-call(s32[4]{0:T(128)S(1)} %fusion.7.index, s32[1,4]{1,0:T(1,128)S(1)} %copy-done.66, f32[2,512,512]{2,1,0:T(8,128)S(1)} %get-tuple-element.175.proj, f32[1,136,128]{2,1,0:T(8,128)S(1)} %bitcast.75, f32[512,384]{1,0:T(8,128)S(1)} %copy-done.97, ...), custom_call_target="tpu_custom_call" | custom-call | flops 2818572288 | bytes 4263936 | tf_op jit(solution)/shard_map/pallas_call | solution.py:327
  194.9 7.2 %shard_map.251 = (f32[512,512]{1,0:T(8,128)S(1)}, f32[136,128]{1,0:T(8,128)S(1)}) custom-call(s32[4]{0:T(128)S(1)} %fusion.5.index, s32[1,4]{1,0:T(1,128)S(1)} %copy-done.66, f32[2,512,512]{2,1,0:T(8,128)S(1)} %get-tuple-element.175.proj, f32[1,136,128]{2,1,0:T(8,128)S(1)} %bitcast.73, f32[512,384]{1,0:T(8,128)S(1)} %copy-done.95, ...), custom_call_target="tpu_custom_call" | custom-call | flops 2818572288 | bytes 4263936 | tf_op jit(solution)/shard_map/pallas_call | solution.py:327
  209.0 7.3 %shard_map.250 = (f32[512,512]{1,0:T(8,128)S(1)}, f32[136,128]{1,0:T(8,128)S(1)}) custom-call(s32[4]{0:T(128)S(1)} %get-tuple-element.318.index, s32[1,4]{1,0:T(1,128)S(1)} %copy-done.66, f32[1,512,512]{2,1,0:T(8,128)S(1)} %bitcast.58, f32[2,136,128]{2,1,0:T(8,128)S(1)} %collective-permute-done.6.carry, f32[512,384]{1,0:T(8,128)S(1)} %copy-done.99, ...), custom_call_target="tpu_custom_call" | custom-call | flops 2818572288 | bytes 3215360 | tf_op jit(solution)/shard_map/pallas_call | solution.py:327
  228.4 4.6 %collective-permute-done.27 = f32[136,128]{1,0:T(8,128)S(1)} collective-permute-done((f32[136,128]{1,0:T(8,128)S(1)}, f32[136,128]{1,0:T(8,128)S(1)}, u32[]{:S(2)}, u32[]{:S(2)}) %collective-permute-start.27) | collective-permute-done | bytes 69664 | tf_op jit(solution)/shard_map/ppermute | solution.py:616
  253.4 5.6 %collective-permute-done.65.refs_5_ = f32[256,512]{1,0:T(8,128)} collective-permute-done((f32[256,512]{1,0:T(8,128)}, f32[256,512]{1,0:T(8,128)}, u32[]{:S(2)}, u32[]{:S(2)}) %collective-permute-start.65) | collective-permute-done | bytes 524320 | tf_op jit(solution)/shard_map/ppermute | solution.py:571
  284.2 5.0 %collective-permute-done.70.refs_6_ = f32[64,512]{1,0:T(8,128)S(1)} collective-permute-done((f32[64,512]{1,0:T(8,128)S(1)}, f32[64,512]{1,0:T(8,128)S(1)}, u32[]{:S(2)}, u32[]{:S(2)}) %collective-permute-start.70) | collective-permute-done | bytes 131104 | tf_op jit(solution)/shard_map/ppermute | solution.py:571
  300.4 7.9 %collective-permute-start.46 = (f32[64,128]{1,0:T(8,128)S(1)}, f32[64,128]{1,0:T(8,128)S(1)}, u32[]{:S(2)}, u32[]{:S(2)}) collective-permute-start(f32[64,128]{1,0:T(8,128)S(1)} %get-tuple-element.252), channel_id=1, source_target_pairs={{0,16},{2,18},{4,20},{6,22},{8,24},{10,26},{12,28},{14,30},{16,0},... | collective-permute-start | bytes 98312 | tf_op jit(solution)/shard_map/ppermute | solution.py:571
  323.0 7.5 %collective-permute-start.53 = (f32[64,128]{1,0:T(8,128)S(1)}, f32[64,128]{1,0:T(8,128)S(1)}, u32[]{:S(2)}, u32[]{:S(2)}) collective-permute-start(f32[64,128]{1,0:T(8,128)S(1)} %get-tuple-element.255.refs_4_), channel_id=1, source_target_pairs={{0,24},{2,26},{4,28},{6,30},{8,16},{10,18},{12,20},{14,22},{16,8},... | collective-permute-start | bytes 98312 | tf_op jit(solution)/shard_map/ppermute | solution.py:571
  330.7 5.0 %collective-permute-done.76.refs_6_ = f32[64,512]{1,0:T(8,128)S(1)} collective-permute-done((f32[64,512]{1,0:T(8,128)S(1)}, f32[64,512]{1,0:T(8,128)S(1)}, u32[]{:S(2)}, u32[]{:S(2)}) %collective-permute-start.76) | collective-permute-done | bytes 131104 | tf_op jit(solution)/shard_map/ppermute | solution.py:571
  335.7 4.6 %collective-permute-start.48 = (f32[64,512]{1,0:T(8,128)S(1)}, f32[64,512]{1,0:T(8,128)S(1)}, u32[]{:S(2)}, u32[]{:S(2)}) collective-permute-start(f32[64,512]{1,0:T(8,128)S(1)} %get-tuple-element.254.refs_0_), channel_id=1, source_target_pairs={{0,8},{2,10},{4,12},{6,14},{8,0},{10,2},{12,4},{14,6},{16,24},{18,... | collective-permute-start | bytes 393224 | tf_op jit(solution)/shard_map/ppermute | solution.py:571
  340.3 5.8 %shard_map.258 = (f32[512,512]{1,0:T(8,128)S(1)}, f32[8,512]{1,0:T(8,128)S(1)}) custom-call(s32[4]{0:T(128)S(1)} %pad_add_fusion.4.scal.idx, f32[512,512]{1,0:T(8,128)S(1)} %bitcast.51, f32[1,512]{1,0:T(1,128)S(1)} %bitcast.78, f32[512,512]{1,0:T(8,128)S(1)} %copy-done.71, f32[512,512]{1,0:T(8,128)S(1)} %copy-done.79, f32[512,512]{1,0:T(8,128)S(1)} %copy-done.77, ...), custom_call_target="tpu_custom_call" | custom-call | flops 3221225472 | bytes 11552768 | tf_op jit(solution)/shard_map/pallas_call | solution.py:50
  347.3 3.9 collective-permute-done.51.refs_5_
  357.2 21.0 %collective-permute-done.86 = f32[4,512]{1,0:T(4,128)S(1)} collective-permute-done((f32[4,512]{1,0:T(4,128)S(1)}, f32[4,512]{1,0:T(4,128)S(1)}, u32[]{:S(2)}, u32[]{:S(2)}) %collective-permute-start.86) | collective-permute-done | bytes 8224 | tf_op jit(solution)/shard_map/ppermute | solution.py:571
  379.2 4.4 %collective-permute-done.89 = f32[4,512]{1,0:T(4,128)S(1)} collective-permute-done((f32[4,512]{1,0:T(4,128)S(1)}, f32[4,512]{1,0:T(4,128)S(1)}, u32[]{:S(2)}, u32[]{:S(2)}) %collective-permute-start.89) | collective-permute-done | bytes 8224 | tf_op jit(solution)/shard_map/ppermute | solution.py:571
  383.7 4.5 %collective-permute-done.88 = f32[4,512]{1,0:T(4,128)S(1)} collective-permute-done((f32[4,512]{1,0:T(4,128)S(1)}, f32[4,512]{1,0:T(4,128)S(1)}, u32[]{:S(2)}, u32[]{:S(2)}) %collective-permute-start.88) | collective-permute-done | bytes 8224 | tf_op jit(solution)/shard_map/ppermute | solution.py:571
  388.2 3.6 collective-permute-done.87
  398.0 4.9 %collective-permute-done.58.o2 = f32[256,128]{1,0:T(8,128)S(1)} collective-permute-done((f32[256,128]{1,0:T(8,128)S(1)}, f32[256,128]{1,0:T(8,128)S(1)}, u32[]{:S(2)}, u32[]{:S(2)}) %collective-permute-start.58) | collective-permute-done | bytes 131104 | tf_op jit(solution)/shard_map/ppermute | solution.py:571
  (427 shorter events, 192.0 us)
Async XLA Ops:
  9.4 45.2 %collective-permute-start.12 = (f32[256,512]{1,0:T(8,128)}, f32[256,512]{1,0:T(8,128)}, u32[]{:S(2)}, u32[]{:S(2)}) collective-permute-start(f32[256,512]{1,0:T(8,128)} %constant_dynamic-slice_fusion), channel_id=1, source_target_pairs={{0,1},{1,0},{2,3},{3,2},{4,5},{5,4},{6,7},{7,6},{8,9},{9,8},{10,11... | collective-permute-start | bytes 1572872 | tf_op jit(solution)/shard_map/ppermute | solution.py:568
  11.3 43.6 %collective-permute-start.11 = (f32[512,256]{1,0:T(8,128)}, f32[512,256]{1,0:T(8,128)}, u32[]{:S(2)}, u32[]{:S(2)}) collective-permute-start(f32[512,256]{1,0:T(8,128)} %constant_dynamic-slice_fusion.1), channel_id=1, source_target_pairs={{0,1},{1,0},{2,3},{3,2},{4,5},{5,4},{6,7},{7,6},{8,9},{9,8},{10,11... | collective-permute-start | bytes 1572872 | tf_op jit(solution)/shard_map/ppermute | solution.py:568
  14.3 30.5 %collective-permute-start.7 = (f32[64,512]{1,0:T(8,128)S(1)}, f32[64,512]{1,0:T(8,128)S(1)}, u32[]{:S(2)}, u32[]{:S(2)}) collective-permute-start(f32[64,512]{1,0:T(8,128)S(1)} %constant_dynamic-slice_fusion.2), channel_id=1, source_target_pairs={{0,1},{1,0},{2,3},{3,2},{4,5},{5,4},{6,7},{7,6},{8,9},{9,8},{10,11... | collective-permute-start | bytes 393224 | tf_op jit(solution)/shard_map/ppermute | solution.py:568
  20.4 38.4 %collective-permute-start.3 = (f32[256,512]{1,0:T(8,128)}, f32[256,512]{1,0:T(8,128)}, u32[]{:S(2)}, u32[]{:S(2)}) collective-permute-start(f32[256,512]{1,0:T(8,128)} %collective-permute-done.wa.a0), channel_id=1, source_target_pairs={{0,4},{2,6},{4,0},{6,2},{8,12},{10,14},{12,8},{14,10},{16,20},{18,... | collective-permute-start | bytes 1572872 | tf_op jit(solution)/shard_map/ppermute | solution.py:571
  54.9 25.2 %collective-permute-start.19 = (f32[512,256]{1,0:T(8,128)}, f32[512,256]{1,0:T(8,128)}, u32[]{:S(2)}, u32[]{:S(2)}) collective-permute-start(f32[512,256]{1,0:T(8,128)} %collective-permute-done.11.u_oth), channel_id=1, source_target_pairs={{0,4},{2,6},{4,0},{6,2},{8,12},{10,14},{12,8},{14,10},{16,20},{18,... | collective-permute-start | bytes 1572872 | tf_op jit(solution)/shard_map/ppermute | solution.py:571
  58.8 30.4 %collective-permute-start.4 = (f32[256,512]{1,0:T(8,128)}, f32[256,512]{1,0:T(8,128)S(1)}, u32[]{:S(2)}, u32[]{:S(2)}) collective-permute-start(f32[256,512]{1,0:T(8,128)} %collective-permute-done.3.wa.a1), channel_id=1, source_target_pairs={{0,2},{2,0},{4,6},{6,4},{8,10},{10,8},{12,14},{14,12},{16,18},{18,... | collective-permute-start | bytes 1572872 | tf_op jit(solution)/shard_map/ppermute | solution.py:571
  64.0 56.4 %collective-permute-start.14 = (f32[256,512]{1,0:T(8,128)}, f32[256,512]{1,0:T(8,128)}, u32[]{:S(2)}, u32[]{:S(2)}) collective-permute-start(f32[256,512]{1,0:T(8,128)} %collective-permute-done.12.d_oth), channel_id=1, source_target_pairs={{0,2},{2,0},{4,6},{6,4},{8,10},{10,8},{12,14},{14,12},{16,18},{18,... | collective-permute-start | bytes 1572872 | tf_op jit(solution)/shard_map/ppermute | solution.py:571
  70.7 39.7 %collective-permute-start.22 = (f32[256,512]{1,0:T(8,128)}, f32[256,512]{1,0:T(8,128)S(1)}, u32[]{:S(2)}, u32[]{:S(2)}) collective-permute-start(f32[256,512]{1,0:T(8,128)} %collective-permute-done.20.d_oth), channel_id=1, source_target_pairs={{0,2},{2,0},{4,6},{6,4},{8,10},{10,8},{12,14},{14,12},{16,18},{18,... | collective-permute-start | bytes 1572872 | tf_op jit(solution)/shard_map/ppermute | solution.py:571
  80.1 30.3 %collective-permute-start.21 = (f32[512,256]{1,0:T(8,128)}, f32[512,256]{1,0:T(8,128)S(1)}, u32[]{:S(2)}, u32[]{:S(2)}) collective-permute-start(f32[512,256]{1,0:T(8,128)} %collective-permute-done.19.u_oth), channel_id=1, source_target_pairs={{0,2},{2,0},{4,6},{6,4},{8,10},{10,8},{12,14},{14,12},{16,18},{18,... | collective-permute-start | bytes 1572872 | tf_op jit(solution)/shard_map/ppermute | solution.py:571
  84.4 36.5 %collective-permute-start.13 = (f32[512,256]{1,0:T(8,128)}, f32[512,256]{1,0:T(8,128)}, u32[]{:S(2)}, u32[]{:S(2)}) collective-permute-start(f32[512,256]{1,0:T(8,128)} %collective-permute-done.11.u_oth), channel_id=1, source_target_pairs={{0,2},{2,0},{4,6},{6,4},{8,10},{10,8},{12,14},{14,12},{16,18},{18,... | collective-permute-start | bytes 1572872 | tf_op jit(solution)/shard_map/ppermute | solution.py:571
  151.5 64.8 %collective-permute-start.61 = (f32[512,256]{1,0:T(8,128)}, f32[512,256]{1,0:T(8,128)}, u32[]{:S(2)}, u32[]{:S(2)}) collective-permute-start(f32[512,256]{1,0:T(8,128)} %get-tuple-element.266), channel_id=1, source_target_pairs={{0,1},{1,0},{2,3},{3,2},{4,5},{5,4},{6,7},{7,6},{8,9},{9,8},{10,11... | collective-permute-start | bytes 1572872 | tf_op jit(solution)/shard_map/ppermute | solution.py:568
  151.6 69.8 %collective-permute-start.62 = (f32[256,512]{1,0:T(8,128)}, f32[256,512]{1,0:T(8,128)}, u32[]{:S(2)}, u32[]{:S(2)}) collective-permute-start(f32[256,512]{1,0:T(8,128)} %get-tuple-element.268), channel_id=1, source_target_pairs={{0,1},{1,0},{2,3},{3,2},{4,5},{5,4},{6,7},{7,6},{8,9},{9,8},{10,11... | collective-permute-start | bytes 1572872 | tf_op jit(solution)/shard_map/ppermute | solution.py:568
  175.5 57.6 %collective-permute-start.32 = (f32[4,256,128]{2,1,0:T(8,128)S(1)}, f32[4,256,128]{2,1,0:T(8,128)S(1)}, u32[]{:S(2)}, u32[]{:S(2)}) collective-permute-start(f32[4,256,128]{2,1,0:T(8,128)S(1)} %get-tuple-element.229), channel_id=1, source_target_pairs={{0,2},{2,0},{4,6},{6,4},{8,10},{10,8},{12,14},{14,12},{16,18},{18,... | collective-permute-start | bytes 1572872 | tf_op jit(solution)/shard_map/ppermute | solution.py:571
  184.6 21.7 %collective-permute-start.28 = (f32[136,128]{1,0:T(8,128)S(1)}, f32[136,128]{1,0:T(8,128)S(1)}, u32[]{:S(2)}, u32[]{:S(2)}) collective-permute-start(f32[136,128]{1,0:T(8,128)S(1)} %get-tuple-element.215), channel_id=1, source_target_pairs={{1,0},{3,2},{5,4},{7,6},{9,8},{11,10},{13,12},{15,14},{17,16},{19,... | collective-permute-start | bytes 208904 | tf_op jit(solution)/shard_map/ppermute | solution.py:616
  206.3 27.3 %collective-permute-start.60 = (f32[512,256]{1,0:T(8,128)S(1)}, f32[512,256]{1,0:T(8,128)S(1)}, u32[]{:S(2)}, u32[]{:S(2)}) collective-permute-start(f32[512,256]{1,0:T(8,128)S(1)} %copy-done.88), channel_id=1, source_target_pairs={{0,1},{1,0},{2,3},{3,2},{4,5},{5,4},{6,7},{7,6},{8,9},{9,8},{10,11... | collective-permute-start | bytes 1572872 | tf_op jit(solution)/shard_map/ppermute | solution.py:568
  209.0 25.1 %collective-permute-start.36 = (f32[256,512]{1,0:T(8,128)S(1)}, f32[256,512]{1,0:T(8,128)S(1)}, u32[]{:S(2)}, u32[]{:S(2)}) collective-permute-start(f32[256,512]{1,0:T(8,128)S(1)} %get-tuple-element.238), channel_id=1, source_target_pairs={{0,2},{2,0},{4,6},{6,4},{8,10},{10,8},{12,14},{14,12},{16,18},{18,... | collective-permute-start | bytes 1572872 | tf_op jit(solution)/shard_map/ppermute | solution.py:571
  216.3 20.9 %collective-permute-start.64 = (f32[256,512]{1,0:T(8,128)S(1)}, f32[256,512]{1,0:T(8,128)S(1)}, u32[]{:S(2)}, u32[]{:S(2)}) collective-permute-start(f32[256,512]{1,0:T(8,128)S(1)} %copy-done.86), channel_id=1, source_target_pairs={{0,1},{1,0},{2,3},{3,2},{4,5},{5,4},{6,7},{7,6},{8,9},{9,8},{10,11... | collective-permute-start | bytes 1572872 | tf_op jit(solution)/shard_map/ppermute | solution.py:568
  234.1 24.9 %collective-permute-start.65 = (f32[256,512]{1,0:T(8,128)}, f32[256,512]{1,0:T(8,128)}, u32[]{:S(2)}, u32[]{:S(2)}) collective-permute-start(f32[256,512]{1,0:T(8,128)} %get-tuple-element.272), channel_id=1, source_target_pairs={{0,4},{2,6},{4,0},{6,2},{8,12},{10,14},{12,8},{14,10},{16,20},{18,... | collective-permute-start | bytes 1572872 | tf_op jit(solution)/shard_map/ppermute | solution.py:571
  238.0 29.9 %collective-permute-start.37 = (f32[256,512]{1,0:T(8,128)}, f32[256,512]{1,0:T(8,128)}, u32[]{:S(2)}, u32[]{:S(2)}) collective-permute-start(f32[256,512]{1,0:T(8,128)} %get-tuple-element.239), channel_id=1, source_target_pairs={{0,1},{1,0},{2,3},{3,2},{4,5},{5,4},{6,7},{7,6},{8,9},{9,8},{10,11... | collective-permute-start | bytes 1572872 | tf_op jit(solution)/shard_map/ppermute | solution.py:568
  238.8 29.1 %collective-permute-start.38 = (f32[256,128]{1,0:T(8,128)}, f32[256,128]{1,0:T(8,128)}, u32[]{:S(2)}, u32[]{:S(2)}) collective-permute-start(f32[256,128]{1,0:T(8,128)} %get-tuple-element.241), channel_id=1, source_target_pairs={{0,1},{1,0},{2,3},{3,2},{4,5},{5,4},{6,7},{7,6},{8,9},{9,8},{10,11... | collective-permute-start | bytes 393224 | tf_op jit(solution)/shard_map/ppermute | solution.py:568
  246.3 44.3 %collective-permute-start.31 = (f32[256,512]{1,0:T(8,128)}, f32[256,512]{1,0:T(8,128)S(1)}, u32[]{:S(2)}, u32[]{:S(2)}) collective-permute-start(f32[256,512]{1,0:T(8,128)} %get-tuple-element.227), channel_id=1, source_target_pairs={{0,2},{2,0},{4,6},{6,4},{8,10},{10,8},{12,14},{14,12},{16,18},{18,... | collective-permute-start | bytes 1572872 | tf_op jit(solution)/shard_map/ppermute | solution.py:571
  267.9 26.3 %collective-permute-start.34 = (f32[256,512]{1,0:T(8,128)S(1)}, f32[256,512]{1,0:T(8,128)S(1)}, u32[]{:S(2)}, u32[]{:S(2)}) collective-permute-start(f32[256,512]{1,0:T(8,128)S(1)} %get-tuple-element.233), channel_id=1, source_target_pairs={{0,1},{1,0},{2,3},{3,2},{4,5},{5,4},{6,7},{7,6},{8,9},{9,8},{10,11... | collective-permute-start | bytes 1572872 | tf_op jit(solution)/shard_map/ppermute | solution.py:568
  269.2 25.0 %collective-permute-start.39 = (f32[256,512]{1,0:T(8,128)S(1)}, f32[256,512]{1,0:T(8,128)S(1)}, u32[]{:S(2)}, u32[]{:S(2)}) collective-permute-start(f32[256,512]{1,0:T(8,128)S(1)} %get-tuple-element.242), channel_id=1, source_target_pairs={{0,4},{2,6},{4,0},{6,2},{8,12},{10,14},{12,8},{14,10},{16,20},{18,... | collective-permute-start | bytes 1572872 | tf_op jit(solution)/shard_map/ppermute | solution.py:571
  294.3 23.4 %collective-permute-start.42 = (f32[64,512]{1,0:T(8,128)S(1)}, f32[64,512]{1,0:T(8,128)S(1)}, u32[]{:S(2)}, u32[]{:S(2)}) collective-permute-start(f32[64,512]{1,0:T(8,128)S(1)} %get-tuple-element.247), channel_id=1, source_target_pairs={{0,8},{2,10},{4,12},{6,14},{8,0},{10,2},{12,4},{14,6},{16,24},{18,... | collective-permute-start | bytes 393224 | tf_op jit(solution)/shard_map/ppermute | solution.py:571
  296.9 21.4 %collective-permute-start.43 = (f32[64,512]{1,0:T(8,128)S(1)}, f32[64,512]{1,0:T(8,128)S(1)}, u32[]{:S(2)}, u32[]{:S(2)}) collective-permute-start(f32[64,512]{1,0:T(8,128)S(1)} %get-tuple-element.248), channel_id=1, source_target_pairs={{0,16},{2,18},{4,20},{6,22},{8,24},{10,26},{12,28},{14,30},{16,0},... | collective-permute-start | bytes 393224 | tf_op jit(solution)/shard_map/ppermute | solution.py:571
  298.4 20.9 %collective-permute-start.44 = (f32[64,512]{1,0:T(8,128)S(1)}, f32[64,512]{1,0:T(8,128)S(1)}, u32[]{:S(2)}, u32[]{:S(2)}) collective-permute-start(f32[64,512]{1,0:T(8,128)S(1)} %get-tuple-element.249), channel_id=1, source_target_pairs={{0,24},{2,26},{4,28},{6,30},{8,16},{10,18},{12,20},{14,22},{16,8},... | collective-permute-start | bytes 393224 | tf_op jit(solution)/shard_map/ppermute | solution.py:571
  323.0 23.3 %collective-permute-start.53 = (f32[64,128]{1,0:T(8,128)S(1)}, f32[64,128]{1,0:T(8,128)S(1)}, u32[]{:S(2)}, u32[]{:S(2)}) collective-permute-start(f32[64,128]{1,0:T(8,128)S(1)} %get-tuple-element.255.refs_4_), channel_id=1, source_target_pairs={{0,24},{2,26},{4,28},{6,30},{8,16},{10,18},{12,20},{14,22},{16,8},... | collective-permute-start | bytes 98312 | tf_op jit(solution)/shard_map/ppermute | solution.py:571
  346.3 45.6 %collective-permute-start.79 = (f32[512,256]{1,0:T(8,128)S(1)}, f32[512,256]{1,0:T(8,128)S(1)}, u32[]{:S(2)}, u32[]{:S(2)}) collective-permute-start(f32[512,256]{1,0:T(8,128)S(1)} %get-tuple-element.283.u0), channel_id=1, source_target_pairs={{0,4},{2,6},{4,0},{6,2},{8,12},{10,14},{12,8},{14,10},{16,20},{18,... | collective-permute-start | bytes 1572872 | tf_op jit(solution)/shard_map/ppermute | solution.py:571
  351.3 41.2 %collective-permute-start.78 = (f32[512,256]{1,0:T(8,128)S(1)}, f32[512,256]{1,0:T(8,128)S(1)}, u32[]{:S(2)}, u32[]{:S(2)}) collective-permute-start(f32[512,256]{1,0:T(8,128)S(1)} %get-tuple-element.283.u0), channel_id=1, source_target_pairs={{0,2},{2,0},{4,6},{6,4},{8,10},{10,8},{12,14},{14,12},{16,18},{18,... | collective-permute-start | bytes 1572872 | tf_op jit(solution)/shard_map/ppermute | solution.py:571
  351.5 40.9 %collective-permute-start.82 = (f32[256,512]{1,0:T(8,128)S(1)}, f32[256,512]{1,0:T(8,128)S(1)}, u32[]{:S(2)}, u32[]{:S(2)}) collective-permute-start(f32[256,512]{1,0:T(8,128)S(1)} %get-tuple-element.284.d0), channel_id=1, source_target_pairs={{0,4},{2,6},{4,0},{6,2},{8,12},{10,14},{12,8},{14,10},{16,20},{18,... | collective-permute-start | bytes 1572872 | tf_op jit(solution)/shard_map/ppermute | solution.py:571
  352.6 40.3 %collective-permute-start.55 = (f32[256,512]{1,0:T(8,128)S(1)}, f32[256,512]{1,0:T(8,128)S(1)}, u32[]{:S(2)}, u32[]{:S(2)}) collective-permute-start(f32[256,512]{1,0:T(8,128)S(1)} %get-tuple-element.256.g0), channel_id=1, source_target_pairs={{0,4},{2,6},{4,0},{6,2},{8,12},{10,14},{12,8},{14,10},{16,20},{18,... | collective-permute-start | bytes 1572872 | tf_op jit(solution)/shard_map/ppermute | solution.py:571
  356.1 22.1 %collective-permute-start.86 = (f32[4,512]{1,0:T(4,128)S(1)}, f32[4,512]{1,0:T(4,128)S(1)}, u32[]{:S(2)}, u32[]{:S(2)}) collective-permute-start(f32[4,512]{1,0:T(4,128)S(1)} %add.54), channel_id=1, source_target_pairs={{0,4},{2,6},{4,0},{6,2},{8,12},{10,14},{12,8},{14,10},{16,20},{18,... | collective-permute-start | bytes 24584 | tf_op jit(solution)/shard_map/ppermute | solution.py:571
  (163 other events, 1938.6 us)
